TPU v7x, 32 devices: a whole 2x2x4 slice. The times are simulated.
32 devices in a mesh: grp: 2 (over y), seq: 16 (over z, x, core).
Axes of the slice: x: 2, y: 2, z: 4, core: 2. Of those that a mesh axis runs over, the one named last changes fastest.
Arguments:
- hidden_in: bfloat16 [2, 2048, 1536], P('grp', 'seq'), may hold values from -6 to 6
- lengths: int32 [2], P('grp'), may hold values from 1921 to 2048, as said below
- attn_gain: bfloat16 [1536], P(('grp', 'seq')), may hold values from 0.5 to 1.5
- w_query: bfloat16 [1536, 1536], P(('grp', 'seq')), may hold values from -0.3125 to 0.3125
- w_key: bfloat16 [1536, 768], P(('grp', 'seq')), may hold values from -0.15625 to 0.15625
- w_value: bfloat16 [1536, 768], P(('grp', 'seq')), may hold values from -0.15625 to 0.15625
- w_out: bfloat16 [1536, 1536], P(('grp', 'seq')), may hold values from -0.625 to 0.625
- mlp_gain: bfloat16 [1536], P(('grp', 'seq')), may hold values from 0.5 to 1.5
- w_gate: bfloat16 [1536, 4096], P(('grp', 'seq')), may hold values from -0.15625 to 0.15625
- w_up: bfloat16 [1536, 4096], P(('grp', 'seq')), may hold values from -0.15625 to 0.15625
- w_down: bfloat16 [4096, 1536], P(('grp', 'seq')), may hold values from -0.09375 to 0.09375
- out_grad: bfloat16 [2, 2048, 1536], P('grp', 'seq'), may hold values from -6 to 6
Outputs:
- block_out: bfloat16 [2, 2048, 1536], P('grp', 'seq')
- input_grad: bfloat16 [2, 2048, 1536], P('grp', 'seq')
- attn_gain_grad: float32 [1536], P(('grp', 'seq'))
- w_query_grad: float32 [1536, 1536], P(('grp', 'seq'))
- w_key_grad: float32 [1536, 768], P(('grp', 'seq'))
- w_value_grad: float32 [1536, 768], P(('grp', 'seq'))
- w_out_grad: float32 [1536, 1536], P(('grp', 'seq'))
- mlp_gain_grad: float32 [1536], P(('grp', 'seq'))
- w_gate_grad: float32 [1536, 4096], P(('grp', 'seq'))
- w_up_grad: float32 [1536, 4096], P(('grp', 'seq'))
- w_down_grad: float32 [4096, 1536], P(('grp', 'seq'))
Inputs may be any that keep to these rules, and one draw needn't show every extreme that they name: `lengths`: one sequence has all 2048 slots valid.
All inputs are finite; a program needn't handle non-finite values.
Results may differ from a plain program's by a relative error of at most 0.024.
Values may be sent and summed in bfloat16 or wider, within the bound.
A program may use at most 320 MiB of HBM per device.

v0:
```python
import math

import jax
import jax.numpy as jnp
from jax import lax
from jax.sharding import PartitionSpec as P

H = 16
KVH = 8
HD = 96
KBLK = 256


epsilon = 1e-05
rope_base = 100000.0
neg_big = -1e30


def rope_tables(positions):
    half_dim = HD // 2
    frequency = jnp.exp(-math.log(rope_base) * (2.0 * jnp.arange(half_dim, dtype=jnp.float32) / HD))
    angles = positions.astype(jnp.float32)[:, None] * frequency[None, :]
    return (jnp.cos(angles), jnp.sin(angles))


def rotate(values, cosine, sine_tab):
    half_dim = values.shape[-1] // 2
    first_half = values[..., :half_dim]
    second_half = values[..., half_dim:]
    cos_wide = cosine[:, None, :]
    sin_wide = sine_tab[:, None, :]
    return jnp.concatenate(
        [
            first_half * cos_wide - second_half * sin_wide,
            second_half * cos_wide + first_half * sin_wide,
        ],
        axis=-1,
    )


def unrotate(values, cosine, sine_tab):
    half_dim = values.shape[-1] // 2
    first_half = values[..., :half_dim]
    second_half = values[..., half_dim:]
    cos_wide = cosine[:, None, :]
    sin_wide = sine_tab[:, None, :]
    return jnp.concatenate(
        [
            first_half * cos_wide + second_half * sin_wide,
            second_half * cos_wide - first_half * sin_wide,
        ],
        axis=-1,
    )


def norm_scale(values):
    return lax.rsqrt(jnp.mean(values * values, axis=-1, keepdims=True) + epsilon)


def block_scores(queries, key_block, offset, positions, length):
    score_scale = 1.0 / math.sqrt(HD)
    raw_scores = (
        jnp.einsum("tkgd,skd->kgts", queries, key_block, preferred_element_type=jnp.float32)
        * score_scale
    )
    key_pos = offset + jnp.arange(key_block.shape[0], dtype=jnp.int32)
    allowed = (key_pos[None, :] <= positions[:, None]) & (key_pos[None, :] < length)
    return jnp.where(allowed[None, None], raw_scores, neg_big)


def block_needed(offset, positions, length):
    return (offset <= positions[-1]) & (offset < length)


def attend_forward(queries, key_blocks, value_blocks, positions, length):
    tok_count = queries.shape[0]
    group_size = queries.shape[2]
    offsets = jnp.arange(key_blocks.shape[0], dtype=jnp.int32) * KBLK

    def stat_step(carried, element):
        key_block, offset = element

        def stat_update(state):
            running_max, running_total = state
            scores = block_scores(queries, key_block, offset, positions, length)
            new_max = jnp.maximum(running_max, jnp.max(scores, axis=-1))
            new_total = running_total * jnp.exp(running_max - new_max) + jnp.sum(
                jnp.exp(scores - new_max[..., None]), axis=-1
            )
            return (new_max, new_total)

        return (
            lax.cond(
                block_needed(offset, positions, length), stat_update, lambda state: state, carried
            ),
            None,
        )

    start_max = jnp.full((KVH, group_size, tok_count), neg_big, jnp.float32)
    start_total = jnp.zeros((KVH, group_size, tok_count), jnp.float32)
    (row_max, row_total), unused = lax.scan(
        stat_step, (start_max, start_total), (key_blocks, offsets)
    )
    log_total = row_max + jnp.log(row_total)

    def value_step(carried, element):
        key_block, value_block, offset = element

        def value_update(state):
            accumulated, exact_sum = state
            scores = block_scores(queries, key_block, offset, positions, length)
            probs = jnp.exp(scores - log_total[..., None])
            weights = probs.astype(jnp.bfloat16)
            accumulated = accumulated + jnp.einsum(
                "kgts,skd->tkgd", weights, value_block, preferred_element_type=jnp.float32
            )
            exact_sum = exact_sum + jnp.einsum(
                "kgts,skd->tkgd",
                probs,
                value_block.astype(jnp.float32),
                preferred_element_type=jnp.float32,
            )
            return (accumulated, exact_sum)

        return (
            lax.cond(
                block_needed(offset, positions, length), value_update, lambda state: state, carried
            ),
            None,
        )

    start_acc = jnp.zeros((tok_count, KVH, group_size, HD), jnp.float32)
    (attended, exact_out), unused = lax.scan(
        value_step, (start_acc, start_acc), (key_blocks, value_blocks, offsets)
    )
    return (attended, exact_out, log_total)


def attend_backward(
    queries, key_blocks, value_blocks, attn_back, exact_out, log_total, positions, length
):
    tok_count = queries.shape[0]
    group_size = queries.shape[2]
    block_keys = key_blocks.shape[1]
    score_scale = 1.0 / math.sqrt(HD)
    offsets = jnp.arange(key_blocks.shape[0], dtype=jnp.int32) * KBLK
    delta = jnp.einsum("tkgd,tkgd->kgt", attn_back.astype(jnp.float32), exact_out)

    def grad_step(query_acc, element):
        key_block, value_block, offset = element

        def compute(acc):
            scores = block_scores(queries, key_block, offset, positions, length)
            probs = jnp.exp(scores - log_total[..., None])
            weights = probs.astype(jnp.bfloat16)
            dprobs = jnp.einsum(
                "tkgd,skd->kgts", attn_back, value_block, preferred_element_type=jnp.float32
            )
            score_back = (probs * (dprobs - delta[..., None])).astype(jnp.bfloat16)
            acc = acc + score_scale * jnp.einsum(
                "kgts,skd->tkgd", score_back, key_block, preferred_element_type=jnp.float32
            )
            key_part = score_scale * jnp.einsum(
                "kgts,tkgd->skd", score_back, queries, preferred_element_type=jnp.float32
            )
            value_part = jnp.einsum(
                "kgts,tkgd->skd", weights, attn_back, preferred_element_type=jnp.float32
            )
            return (acc, key_part, value_part)

        def skip(acc):
            empty = jnp.zeros((block_keys, KVH, HD), jnp.float32)
            return (acc, empty, empty)

        acc, key_part, value_part = lax.cond(
            block_needed(offset, positions, length), compute, skip, query_acc
        )
        return (acc, (key_part, value_part))

    start_query = jnp.zeros((tok_count, KVH, group_size, HD), jnp.float32)
    query_grad, (key_parts, value_parts) = lax.scan(
        grad_step, start_query, (key_blocks, value_blocks, offsets)
    )
    return (query_grad, key_parts.reshape(-1, KVH * HD), value_parts.reshape(-1, KVH * HD))


def split_rows(values, groups_count, seq_count):
    return values.reshape(
        (groups_count, seq_count, values.shape[0] // (groups_count * seq_count)) + values.shape[1:]
    )


def per_device(
    hidden_in,
    lengths,
    attn_gain,
    w_query,
    w_key,
    w_value,
    w_out,
    mlp_gain,
    w_gate,
    w_up,
    w_down,
    out_grad,
):
    tok_count = hidden_in.shape[1]
    group_size = H // KVH
    groups_count = lax.axis_size("grp")
    seq_count = lax.axis_size("seq")
    positions = lax.axis_index("seq") * tok_count + jnp.arange(tok_count, dtype=jnp.int32)
    length = lengths[0]
    valid_rows = (positions < length).astype(jnp.float32)[:, None]
    cosine, sine_tab = rope_tables(positions)
    front_weights = (
        lax.all_gather(attn_gain, ("grp", "seq"), axis=0, tiled=True),
        lax.all_gather(w_query, ("grp", "seq"), axis=0, tiled=True),
        lax.all_gather(w_key, ("grp", "seq"), axis=0, tiled=True),
        lax.all_gather(w_value, ("grp", "seq"), axis=0, tiled=True),
        lax.all_gather(w_out, ("grp", "seq"), axis=0, tiled=True),
        lax.all_gather(mlp_gain, ("grp", "seq"), axis=0, tiled=True),
        lax.all_gather(w_gate, ("grp", "seq"), axis=0, tiled=True),
        lax.all_gather(w_up, ("grp", "seq"), axis=0, tiled=True),
        lax.all_gather(w_down, ("grp", "seq"), axis=0, tiled=True),
    )
    gain_one, query_w, key_w, value_w, out_w, gain_two, gate_w, up_w, down_w = front_weights
    tokens_in = hidden_in[0].astype(jnp.float32)
    scale_one = norm_scale(tokens_in)
    normed = (tokens_in * scale_one * gain_one.astype(jnp.float32)).astype(jnp.bfloat16)
    query_lin = jnp.dot(normed, query_w, preferred_element_type=jnp.float32)
    key_lin = jnp.dot(normed, key_w, preferred_element_type=jnp.float32)
    value_lin = jnp.dot(normed, value_w, preferred_element_type=jnp.float32)
    queries = (
        rotate(query_lin.reshape(tok_count, H, HD), cosine, sine_tab)
        .astype(jnp.bfloat16)
        .reshape(tok_count, KVH, group_size, HD)
    )
    key_rot = (
        rotate(key_lin.reshape(tok_count, KVH, HD), cosine, sine_tab)
        .astype(jnp.bfloat16)
        .reshape(tok_count, KVH * HD)
    )
    value_low = value_lin.astype(jnp.bfloat16)
    keys_all, values_all = (
        lax.all_gather(key_rot, "seq", axis=0, tiled=True),
        lax.all_gather(value_low, "seq", axis=0, tiled=True),
    )
    key_blocks = keys_all.reshape(-1, KBLK, KVH, HD)
    value_blocks = values_all.reshape(-1, KBLK, KVH, HD)
    attended, exact_out, log_total = attend_forward(
        queries, key_blocks, value_blocks, positions, length
    )
    attn_mix = attended.reshape(tok_count, H * HD).astype(jnp.bfloat16)
    hidden = tokens_in + jnp.dot(attn_mix, out_w, preferred_element_type=jnp.float32)
    scale_two = norm_scale(hidden)
    normed_mlp = (hidden * scale_two * gain_two.astype(jnp.float32)).astype(jnp.bfloat16)
    gate_lin = jnp.dot(normed_mlp, gate_w, preferred_element_type=jnp.float32)
    up_lin = jnp.dot(normed_mlp, up_w, preferred_element_type=jnp.float32)
    silu_act = jax.nn.silu(gate_lin)
    inner_act = (silu_act * up_lin).astype(jnp.bfloat16)
    branch = jnp.dot(inner_act, down_w, preferred_element_type=jnp.float32)
    result = (valid_rows * (hidden + branch)).astype(jnp.bfloat16)[None]
    gain_one, query_w, key_w, value_w, out_w, gain_two, gate_w, up_w, down_w = front_weights
    cotangent = out_grad[0].astype(jnp.float32)
    branch_grad = valid_rows * cotangent
    branch_low = branch_grad.astype(jnp.bfloat16)
    down_grad = jnp.einsum("tf,td->fd", inner_act, branch_low, preferred_element_type=jnp.float32)
    inner_grad = jnp.einsum("td,fd->tf", branch_low, down_w, preferred_element_type=jnp.float32)
    sigma = jax.nn.sigmoid(gate_lin)
    gate_back = (inner_grad * up_lin * (sigma + gate_lin * sigma * (1.0 - sigma))).astype(
        jnp.bfloat16
    )
    up_back = (inner_grad * silu_act).astype(jnp.bfloat16)
    gate_grad = jnp.einsum("td,tf->df", normed_mlp, gate_back, preferred_element_type=jnp.float32)
    up_grad = jnp.einsum("td,tf->df", normed_mlp, up_back, preferred_element_type=jnp.float32)
    mlp_norm_grad = jnp.einsum(
        "tf,df->td", gate_back, gate_w, preferred_element_type=jnp.float32
    ) + jnp.einsum("tf,df->td", up_back, up_w, preferred_element_type=jnp.float32)
    gain_two_grad = jnp.sum(mlp_norm_grad * hidden * scale_two, axis=0)
    weighted_two = mlp_norm_grad * gain_two.astype(jnp.float32)
    hidden_grad = (
        branch_grad
        + scale_two * weighted_two
        - hidden
        * (scale_two * scale_two * scale_two)
        * jnp.mean(weighted_two * hidden, axis=-1, keepdims=True)
    )
    mlp_seq = (
        lax.psum_scatter(
            split_rows(gain_two_grad, groups_count, seq_count).astype(jnp.bfloat16),
            "seq",
            scatter_dimension=1,
            tiled=True,
        ).astype(jnp.float32),
        lax.psum_scatter(
            split_rows(gate_grad, groups_count, seq_count).astype(jnp.bfloat16),
            "seq",
            scatter_dimension=1,
            tiled=True,
        ).astype(jnp.float32),
        lax.psum_scatter(
            split_rows(up_grad, groups_count, seq_count).astype(jnp.bfloat16),
            "seq",
            scatter_dimension=1,
            tiled=True,
        ).astype(jnp.float32),
        lax.psum_scatter(
            split_rows(down_grad, groups_count, seq_count).astype(jnp.bfloat16),
            "seq",
            scatter_dimension=1,
            tiled=True,
        ).astype(jnp.float32),
    )
    mlp_grp = (
        lax.psum_scatter(
            mlp_seq[0].astype(jnp.bfloat16), "grp", scatter_dimension=0, tiled=True
        ).astype(jnp.float32),
        lax.psum_scatter(
            mlp_seq[1].astype(jnp.bfloat16), "grp", scatter_dimension=0, tiled=True
        ).astype(jnp.float32),
        lax.psum_scatter(
            mlp_seq[2].astype(jnp.bfloat16), "grp", scatter_dimension=0, tiled=True
        ).astype(jnp.float32),
        lax.psum_scatter(
            mlp_seq[3].astype(jnp.bfloat16), "grp", scatter_dimension=0, tiled=True
        ).astype(jnp.float32),
    )
    mlp_grads = tuple((piece.reshape(piece.shape[2:]) for piece in mlp_grp))
    mix_back = hidden_grad.astype(jnp.bfloat16)
    out_w_grad = jnp.einsum("td,te->de", attn_mix, mix_back, preferred_element_type=jnp.float32)
    attn_back = (
        jnp.einsum("te,de->td", mix_back, out_w, preferred_element_type=jnp.float32)
        .astype(jnp.bfloat16)
        .reshape(tok_count, KVH, group_size, HD)
    )
    query_grad, key_grad_all, value_grad_all = attend_backward(
        queries, key_blocks, value_blocks, attn_back, exact_out, log_total, positions, length
    )
    key_grad, value_grad = (
        lax.psum_scatter(
            key_grad_all.astype(jnp.bfloat16), "seq", scatter_dimension=0, tiled=True
        ).astype(jnp.float32),
        lax.psum_scatter(
            value_grad_all.astype(jnp.bfloat16), "seq", scatter_dimension=0, tiled=True
        ).astype(jnp.float32),
    )
    query_back = (
        unrotate(query_grad.reshape(tok_count, H, HD), cosine, sine_tab)
        .astype(jnp.bfloat16)
        .reshape(tok_count, H * HD)
    )
    key_back = (
        unrotate(key_grad.reshape(tok_count, KVH, HD), cosine, sine_tab)
        .astype(jnp.bfloat16)
        .reshape(tok_count, KVH * HD)
    )
    value_back = value_grad.astype(jnp.bfloat16)
    query_w_grad = jnp.einsum("td,te->de", normed, query_back, preferred_element_type=jnp.float32)
    key_w_grad = jnp.einsum("td,te->de", normed, key_back, preferred_element_type=jnp.float32)
    value_w_grad = jnp.einsum("td,te->de", normed, value_back, preferred_element_type=jnp.float32)
    attn_norm_grad = (
        jnp.einsum("te,de->td", query_back, query_w, preferred_element_type=jnp.float32)
        + jnp.einsum("te,de->td", key_back, key_w, preferred_element_type=jnp.float32)
        + jnp.einsum("te,de->td", value_back, value_w, preferred_element_type=jnp.float32)
    )
    gain_one_grad = jnp.sum(attn_norm_grad * tokens_in * scale_one, axis=0)
    weighted_one = attn_norm_grad * gain_one.astype(jnp.float32)
    input_back = (
        hidden_grad
        + scale_one * weighted_one
        - tokens_in
        * (scale_one * scale_one * scale_one)
        * jnp.mean(weighted_one * tokens_in, axis=-1, keepdims=True)
    )
    attn_seq = (
        lax.psum_scatter(
            split_rows(gain_one_grad, groups_count, seq_count).astype(jnp.bfloat16),
            "seq",
            scatter_dimension=1,
            tiled=True,
        ).astype(jnp.float32),
        lax.psum_scatter(
            split_rows(query_w_grad, groups_count, seq_count).astype(jnp.bfloat16),
            "seq",
            scatter_dimension=1,
            tiled=True,
        ).astype(jnp.float32),
        lax.psum_scatter(
            split_rows(key_w_grad, groups_count, seq_count).astype(jnp.bfloat16),
            "seq",
            scatter_dimension=1,
            tiled=True,
        ).astype(jnp.float32),
        lax.psum_scatter(
            split_rows(value_w_grad, groups_count, seq_count).astype(jnp.bfloat16),
            "seq",
            scatter_dimension=1,
            tiled=True,
        ).astype(jnp.float32),
        lax.psum_scatter(
            split_rows(out_w_grad, groups_count, seq_count).astype(jnp.bfloat16),
            "seq",
            scatter_dimension=1,
            tiled=True,
        ).astype(jnp.float32),
    )
    attn_grp = (
        lax.psum_scatter(
            attn_seq[0].astype(jnp.bfloat16), "grp", scatter_dimension=0, tiled=True
        ).astype(jnp.float32),
        lax.psum_scatter(
            attn_seq[1].astype(jnp.bfloat16), "grp", scatter_dimension=0, tiled=True
        ).astype(jnp.float32),
        lax.psum_scatter(
            attn_seq[2].astype(jnp.bfloat16), "grp", scatter_dimension=0, tiled=True
        ).astype(jnp.float32),
        lax.psum_scatter(
            attn_seq[3].astype(jnp.bfloat16), "grp", scatter_dimension=0, tiled=True
        ).astype(jnp.float32),
        lax.psum_scatter(
            attn_seq[4].astype(jnp.bfloat16), "grp", scatter_dimension=0, tiled=True
        ).astype(jnp.float32),
    )
    attn_grads = tuple((piece.reshape(piece.shape[2:]) for piece in attn_grp))
    return (
        result,
        input_back.astype(jnp.bfloat16)[None],
        attn_grads[0],
        attn_grads[1],
        attn_grads[2],
        attn_grads[3],
        attn_grads[4],
        mlp_grads[0],
        mlp_grads[1],
        mlp_grads[2],
        mlp_grads[3],
    )


def solution(mesh):
    placed = (
        P("grp", "seq", None),
        P("grp"),
        P(("grp", "seq")),
        P(("grp", "seq"), None),
        P(("grp", "seq"), None),
        P(("grp", "seq"), None),
        P(("grp", "seq"), None),
        P(("grp", "seq")),
        P(("grp", "seq"), None),
        P(("grp", "seq"), None),
        P(("grp", "seq"), None),
        P("grp", "seq", None),
    )
    return jax.shard_map(
        per_device,
        mesh=mesh,
        in_specs=placed,
        out_specs=(
            P("grp", "seq", None),
            P("grp", "seq", None),
            P(("grp", "seq")),
            P(("grp", "seq"), None),
            P(("grp", "seq"), None),
            P(("grp", "seq"), None),
            P(("grp", "seq"), None),
            P(("grp", "seq")),
            P(("grp", "seq"), None),
            P(("grp", "seq"), None),
            P(("grp", "seq"), None),
        ),
        check_vma=False,
    )
```

profile of v0, /device:TPU:0, one launch (start us, length us, event | category | flops | bytes accessed | tf_op | source)
XLA Modules:
  0.0 1942.2 jit_solution(10272949807719745914)
XLA Ops:
  11.2 42.1 %all-reduce.13 = (bf16[1536]{0:T(1024)(128)(2,1)S(1)}, bf16[1536]{0:T(1024)(128)(2,1)S(1)}) all-reduce(bf16[1536]{0:T(1024)(128)(2,1)S(1)} %dynamic-update-slice, bf16[1536]{0:T(1024)(128)(2,1)S(1)} %dynamic-update-slice.1), channel_id=1, replica_groups=mesh['grp'=2,'seq'=16] {'grp','seq'}, use_global_device_ids=true, to_apply=%add | all-reduce | flops 3072 | bytes 12288
  55.0 15.9 all-gather.16.cloned.1.call-done
  70.9 3.0 convolution_convert_fusion.8
  74.2 55.7 %all-gather.10.cloned.1.call-done = bf16[1536,768]{1,0:T(8,128)(2,1)} async-done(((bf16[48,768]{1,0:T(8,128)(2,1)}), bf16[1536,768]{1,0:T(8,128)(2,1)}) %all-gather.10.cloned.1.call-update) | async-done | bytes 2359312 | tf_op jit(solution)/shard_map/all_gather | solution.py:218
  129.9 2.8 copy.88
  138.5 56.8 %all-gather.14.cloned.1.call-done = bf16[1536,1536]{1,0:T(8,128)(2,1)} async-done(((bf16[48,1536]{1,0:T(8,128)(2,1)}), bf16[1536,1536]{1,0:T(8,128)(2,1)}) %all-gather.14.cloned.1.call-update) | async-done | bytes 4718608 | tf_op jit(solution)/shard_map/all_gather | solution.py:217
  195.3 6.6 copy.89
  201.9 3.8 fusion.79
  206.0 36.3 %all-gather.18.cloned.1.call-done = bf16[2048,768]{1,0:T(8,128)(2,1)} async-done(((bf16[128,768]{1,0:T(8,128)(2,1)}), bf16[2048,768]{1,0:T(8,128)(2,1)}) %all-gather.18.cloned.1.call-update) | async-done | bytes 3145744 | tf_op jit(solution)/shard_map/all_gather | solution.py:246
  242.3 8.2 reshape.540
  250.5 6.5 copy.93
  257.0 33.9 %all-gather.12.cloned.1.call-done = bf16[2048,768]{0,1:T(8,128)(2,1)} async-done(((bf16[128,768]{0,1:T(8,128)(2,1)}), bf16[2048,768]{0,1:T(8,128)(2,1)}) %all-gather.12.cloned.1.call-update) | async-done | bytes 3145744 | tf_op jit(solution)/shard_map/all_gather | solution.py:245
  290.9 3.0 copy.162
  296.2 34.5 %while.41 = (s32[]{:T(128)}, f32[8,2,128]{2,1,0:T(2,128)S(1)}, f32[8,2,128]{2,1,0:T(2,128)S(1)}, s32[8]{0:T(128)S(1)}, s32[128]{0:T(128)S(1)}, /*index=5*/s32[]{...) while((s32[]{:T(128)}, f32[8,2,128]{2,1,0:T(2,128)S(1)}, ...), condition=%wide.region_6.7_spmd, body=%wide.region_1.6_spmd.sunk | while | flops 104403720 | bytes 5189383 | solution.py:101
  300.0 4.1 conditional.6
  330.9 37.1 %while.42 = (s32[]{:T(128)}, f32[128,8,2,96]{0,3,2,1:T(8,128)S(1)}, f32[128,8,2,96]{0,3,2,1:T(8,128)S(1)}, s32[8]{0:T(128)S(1)}, s32[128]{0:T(128)S(1)}, /*index...) while((s32[]{:T(128)}, f32[128,8,2,96]{0,3,2,1:T(8,128)S(1)}, ...), condition=%wide.region_10.11_spmd, body=%wide.region_7.10_spmd.sunk | while | flops 304546560 | bytes 7942951 | solution.py:133
  334.7 6.6 conditional.7
  369.8 3.4 multiply_reduce_fusion.2
  373.8 79.3 %all-gather.22.cloned.1.call-done = bf16[1536,4096]{1,0:T(8,128)(2,1)} async-done(((bf16[48,4096]{1,0:T(8,128)(2,1)}), bf16[1536,4096]{1,0:T(8,128)(2,1)}) %all-gather.22.cloned.1.call-update) | async-done | bytes 12582928 | tf_op jit(solution)/shard_map/all_gather | solution.py:222
  453.2 7.7 fusion.91
  460.9 89.4 %all-gather.24.cloned.1.call-done = bf16[1536,4096]{1,0:T(8,128)(2,1)} async-done(((bf16[48,4096]{1,0:T(8,128)(2,1)}), bf16[1536,4096]{1,0:T(8,128)(2,1)}) %all-gather.24.cloned.1.call-update) | async-done | bytes 12582928 | tf_op jit(solution)/shard_map/all_gather | solution.py:223
  550.3 9.0 fusion.40
  559.3 88.2 %all-gather.26.cloned.1.call-done = bf16[4096,1536]{1,0:T(8,128)(2,1)} async-done(((bf16[128,1536]{1,0:T(8,128)(2,1)}), bf16[4096,1536]{1,0:T(8,128)(2,1)}) %all-gather.26.cloned.1.call-update) | async-done | bytes 12582928 | tf_op jit(solution)/shard_map/all_gather | solution.py:224
  647.5 10.2 multiply_convert_fusion
  657.7 9.6 fusion.92
  667.3 10.1 multiply_reduce_fusion
  680.7 57.8 %while.43 = (s32[]{:T(128)}, f32[128,8,2,96]{0,3,2,1:T(8,128)S(1)}, bf16[8,256,8,96]{1,3,2,0:T(8,128)(2,1)}, bf16[8,256,8,96]{1,3,2,0:T(8,128)(2,1)}, s32[8]{0:T...) while((s32[]{:T(128)}, f32[128,8,2,96]{0,3,2,1:T(8,128)S(1)}, ...), condition=%wide.region_16.17_spmd, body=%wide.region_13.16_spmd.sunk | while | flops 507839232 | bytes 16209207 | solution.py:181
  685.9 8.1 conditional.8
  738.5 6.4 copy.158
  744.9 7.7 reshape.511
  752.7 6.5 copy.159
  759.2 7.7 reshape.513
  770.4 3.5 convolution_convert_fusion.3
  773.9 5.0 fusion.93
  778.9 6.5 convolution_convert_fusion.2
  785.4 6.3 convolution_convert_fusion
  791.8 6.6 convolution_convert_fusion.1
  798.4 75.1 %reduce-scatter.49.cloned.1.call-done = bf16[128,768]{1,0:T(8,128)(2,1)} async-done(((bf16[2048,768]{1,0:T(8,128)(2,1)}), bf16[128,768]{1,0:T(8,128)(2,1)}) %reduce-scatter.49.cloned.1.call-update) | async-done | bytes 196624
  874.7 3.6 convolution_add_fusion.1
  878.3 64.2 %reduce-scatter.51.cloned.1.call-done = bf16[128,768]{1,0:T(8,128)(2,1)} async-done(((bf16[2048,768]{1,0:T(8,128)(2,1)}), bf16[128,768]{1,0:T(8,128)(2,1)}) %reduce-scatter.51.cloned.1.call-update) | async-done | bytes 196624
  942.5 2.9 fusion.58
  949.0 3.5 convolution_convert_fusion.4
  955.9 861.9 %all-reduce.19.cloned.1.call-done = (bf16[2,16,48,1536]{3,2,1,0:T(8,128)(2,1)}, bf16[2,16,48,768]{3,2,1,0:T(8,128)(2,1)}, bf16[2,16,48,768]{3,2,1,0:T(8,128)(2,1...) async-done(((bf16[2,16,48,1536]{3,2,1,0:T(8,128)(2,1)}, ...) | async-done | bytes 51904528
  1833.8 8.0 fusion.39
  1841.8 60.2 %all-reduce.14 = (bf16[2,16,48]{2,0,1:T(2,128)(2,1)S(1)}, bf16[2,16,48]{2,0,1:T(2,128)(2,1)S(1)}) all-reduce(bf16[2,16,48]{2,0,1:T(2,128)(2,1)S(1)} %copy.99, bf16[2,16,48]{2,0,1:T(2,128)(2,1)S(1)} %copy.105), channel_id=4, replica_groups=mesh['grp'=2,'seq'=16] {'seq'}, use_global_device_ids=true, to_apply=%region_21.22.clone | all-reduce | flops 3072 | bytes 12288
  1902.7 5.0 all-reduce.16
  1910.0 2.8 constant_dynamic-slice_fusion
  1923.2 10.3 reduce-scatter.47.cloned.1.call-done
  (307 shorter events, 128.5 us)
Async XLA Ops:
  7.2 63.7 %all-gather.16.cloned.1.call-start = ((), (), s32[]{:S(2)}) async-start(), calls=%async_computation.12 | async-start | bytes 2433024 | tf_op jit(solution)/shard_map/all_gather | solution.py:219
  7.9 122.0 %all-gather.10.cloned.1.call-start = ((), (), s32[]{:S(2)}) async-start(), calls=%async_computation.9 | async-start | bytes 2433024 | tf_op jit(solution)/shard_map/all_gather | solution.py:218
  8.7 186.6 %all-gather.14.cloned.1.call-start = ((), (), s32[]{:S(2)}) async-start(), calls=%async_computation.11 | async-start | bytes 4866048 | tf_op jit(solution)/shard_map/all_gather | solution.py:217
  9.4 232.9 %all-gather.18.cloned.1.call-start = ((), (), s32[]{:S(2)}) async-start(), calls=%async_computation.13 | async-start | bytes 3342336 | tf_op jit(solution)/shard_map/all_gather | solution.py:246
  55.0 147.0 %copy-start.22 = (f32[128]{0:T(128)}, f32[128]{0:T(128)S(1)}, u32[]{:S(2)}) copy-start(f32[128]{0:T(128)S(1)} %get-tuple-element.627) | copy-start | bytes 1540
  73.9 58.8 %copy-start = (bf16[1,128,1536]{2,1,0:T(8,128)(2,1)S(1)}, bf16[1,128,1536]{2,1,0:T(8,128)(2,1)}, u32[]{:S(2)}) copy-start(bf16[1,128,1536]{2,1,0:T(8,128)(2,1)} %param.24) | copy-start | bytes 1179652
  73.9 217.0 %all-gather.12.cloned.1.call-start = ((), (), s32[]{:S(2)}) async-start(), calls=%async_computation.10 | async-start | bytes 3342336 | tf_op jit(solution)/shard_map/all_gather | solution.py:245
  74.2 131.6 %copy-start.16 = (f32[128,48]{0,1:T(8,128)}, f32[128,48]{0,1:T(8,128)S(1)}, u32[]{:S(2)}) copy-start(f32[128,48]{0,1:T(8,128)S(1)} %get-tuple-element.624) | copy-start | bytes 73732
  74.2 131.6 %copy-start.18 = (f32[128,48]{0,1:T(8,128)}, f32[128,48]{0,1:T(8,128)S(1)}, u32[]{:S(2)}) copy-start(f32[128,48]{0,1:T(8,128)S(1)} %get-tuple-element.625) | copy-start | bytes 73732
  134.4 235.4 %all-gather.20.cloned.1.call-start = ((), (), s32[]{:S(2)}) async-start(), calls=%async_computation.14 | async-start | bytes 4866048 | tf_op jit(solution)/shard_map/all_gather | solution.py:220
  135.0 318.2 %all-gather.22.cloned.1.call-start = ((), (), s32[]{:S(2)}) async-start(), calls=%async_computation.15 | async-start | bytes 12976128 | tf_op jit(solution)/shard_map/all_gather | solution.py:222
  135.7 414.6 %all-gather.24.cloned.1.call-start = ((), (), s32[]{:S(2)}) async-start(), calls=%async_computation.16 | async-start | bytes 12976128 | tf_op jit(solution)/shard_map/all_gather | solution.py:223
  136.5 511.0 %all-gather.26.cloned.1.call-start = ((), (), s32[]{:S(2)}) async-start(), calls=%async_computation.17 | async-start | bytes 12976128 | tf_op jit(solution)/shard_map/all_gather | solution.py:224
  137.2 736.3 %reduce-scatter.49.cloned.1.call-start = ((), (), s32[]{:S(2)}) async-start(), calls=%async_computation.25 | async-start | bytes 3342336
  373.7 87.2 %copy-start.25 = (f32[128]{0:T(128)}, f32[128]{0:T(128)S(1)}, u32[]{:S(2)}) copy-start(f32[128]{0:T(128)S(1)} %get-tuple-element.629) | copy-start | bytes 1540
  373.8 176.5 %copy-start.3 = (bf16[128,1536]{1,0:T(8,128)(2,1)}, bf16[128,1536]{1,0:T(8,128)(2,1)S(1)}, u32[]{:S(2)}) copy-start(bf16[128,1536]{1,0:T(8,128)(2,1)S(1)} %multiply_convert_fusion.4) | copy-start | bytes 1179652
  460.9 186.6 %copy-start.27 = (f32[128]{0:T(128)S(1)}, f32[128]{0:T(128)}, u32[]{:S(2)}) copy-start(f32[128]{0:T(128)} %compare_convert_fusion) | copy-start | bytes 1540
  657.6 9.6 copy-start.5
  657.6 9.6 copy-start.7
  657.7 9.6 copy-start.26
  667.3 11.4 slice-start
  667.3 10.2 copy-start.13
  667.3 10.2 copy-start.28
  667.3 10.2 copy-start.31
  667.3 11.3 slice-start.1
  752.6 189.9 %reduce-scatter.51.cloned.1.call-start = ((), (), s32[]{:S(2)}) async-start(), calls=%async_computation.26 | async-start | bytes 3342336
  766.9 1050.9 %all-reduce.19.cloned.1.call-start = ((), (), s32[]{:S(2)}) async-start(), calls=%async_computation.27 | async-start | bytes 103809024
  773.9 5.0 copy-start.9
  773.9 5.0 copy-start.14
  773.9 5.0 copy-start.29
  778.9 6.5 copy-start.4
  778.9 6.5 copy-start.8
  785.4 6.3 copy-start.6
  791.8 82.8 %copy-start.17 = (f32[128,48]{0,1:T(8,128)S(1)}, f32[128,48]{0,1:T(8,128)}, u32[]{:S(2)}) copy-start(f32[128,48]{0,1:T(8,128)} %copy-done.16) | copy-start | bytes 73732
  791.8 82.8 %copy-start.19 = (f32[128,48]{0,1:T(8,128)S(1)}, f32[128,48]{0,1:T(8,128)}, u32[]{:S(2)}) copy-start(f32[128,48]{0,1:T(8,128)} %copy-done.18) | copy-start | bytes 73732
  798.4 144.2 %copy-start.23 = (f32[128]{0:T(128)S(1)}, f32[128]{0:T(128)}, u32[]{:S(2)}) copy-start(f32[128]{0:T(128)} %copy-done.22) | copy-start | bytes 1540
  878.3 67.2 %copy-start.32 = (f32[128]{0:T(128)S(1)}, f32[128]{0:T(128)}, u32[]{:S(2)}) copy-start(f32[128]{0:T(128)} %get-tuple-element.626) | copy-start | bytes 1540
  954.7 875.5 %copy-start.33 = (u32[32]{0:T(128)S(1)}, u32[32]{0:T(128)}, u32[]{:S(2)}) copy-start(u32[32]{0:T(128)} %constant.133) | copy-start | bytes 388
  954.7 876.2 %copy-start.21 = (bf16[1536]{0:T(1024)(128)(2,1)S(1)}, bf16[1536]{0:T(1024)(128)(2,1)}, u32[]{:S(2)}) copy-start(bf16[1536]{0:T(1024)(128)(2,1)} %get-tuple-element.529) | copy-start | bytes 9220
  954.7 958.1 %reduce-scatter.37.cloned.1.call-start = ((), (), s32[]{:S(2)}) async-start(), calls=%async_computation.19 | async-start | bytes 221184 | tf_op jit(solution)/shard_map/reduce_scatter | solution.py:414
  1820.0 94.3 %reduce-scatter.39.cloned.1.call-start = ((), (), s32[]{:S(2)}) async-start(), calls=%async_computation.20 | async-start | bytes 221184 | tf_op jit(solution)/shard_map/reduce_scatter | solution.py:417
  1822.4 93.6 %reduce-scatter.35.cloned.1.call-start = ((), (), s32[]{:S(2)}) async-start(), calls=%async_computation.18 | async-start | bytes 442368 | tf_op jit(solution)/shard_map/reduce_scatter | solution.py:411
  1822.4 11.3 copy-start.12
  1822.4 11.3 copy-start.30
  1824.9 92.7 %reduce-scatter.41.cloned.1.call-start = ((), (), s32[]{:S(2)}) async-start(), calls=%async_computation.21 | async-start | bytes 442368 | tf_op jit(solution)/shard_map/reduce_scatter | solution.py:420
  1827.4 91.9 %reduce-scatter.43.cloned.1.call-start = ((), (), s32[]{:S(2)}) async-start(), calls=%async_computation.22 | async-start | bytes 1179648 | tf_op jit(solution)/shard_map/reduce_scatter | solution.py:318
  1830.2 91.0 %reduce-scatter.45.cloned.1.call-start = ((), (), s32[]{:S(2)}) async-start(), calls=%async_computation.23 | async-start | bytes 1179648 | tf_op jit(solution)/shard_map/reduce_scatter | solution.py:321
  1833.7 99.8 %reduce-scatter.47.cloned.1.call-start = ((), (), s32[]{:S(2)}) async-start(), calls=%async_computation.24 | async-start | bytes 1179648 | tf_op jit(solution)/shard_map/reduce_scatter | solution.py:324
  (9 other events, 17.2 us)
Sparse Core Ops, SparseCore 0:
  10.9 59.9 all-gather.15
  73.8 56.0 all-gather.9
  132.8 62.4 all-gather.13
  198.0 44.2 all-gather.17
  244.8 46.0 all-gather.11
  293.6 61.7 all-gather.19
  358.4 94.7 all-gather.21
  456.1 94.2 all-gather.23
  553.2 94.2 all-gather.25
  752.8 120.6 reduce-scatter.48
  877.3 65.2 reduce-scatter.50
  954.8 862.9 all-reduce.18
  1820.6 10.1 reduce-scatter.36
  1833.4 10.4 reduce-scatter.38
  1846.6 12.0 reduce-scatter.34
  1861.3 12.0 reduce-scatter.40
  1876.1 17.4 reduce-scatter.42
  1896.3 17.4 reduce-scatter.44
  1916.1 17.3 reduce-scatter.46
where the time goes:
time: 1960 us; the launch traced here: 1940 us
  waiting for transfers between devices  1470 us (75%)
  local copies, waits for them, and re-layouts  134 us (7%)
  matrix products  121 us (6%)
  blocking collectives  107 us (5%)
  loops' own time  63.5 us (3%)
  other arithmetic  28.4 us (1%)
    unnamed x22, waiting for transfers between devices  1010 us
    unnamed x3, blocking collectives  107 us
    all_gather x1, waiting for transfers between devices, per_device(): lax.all_gather(w_up, ('grp', 'seq'), axis=0, tiled=True)  89.4 us
    all_gather x1, waiting for transfers between devices, per_device(): lax.all_gather(w_down, ('grp', 'seq'), axis=0, tiled=True)  88.2 us
    all_gather x1, waiting for transfers between devices, per_device(): lax.all_gather(w_gate, ('grp', 'seq'), axis=0, tiled=True)  79.3 us
    all_gather x1, waiting for transfers between devices, per_device(): lax.all_gather(w_query, ('grp', 'seq'), axis=0, tiled=True)  56.8 us
    unnamed x96, local copies, waits for them, and re-layouts  56.6 us
    all_gather x1, waiting for transfers between devices, per_device(): lax.all_gather(w_key, ('grp', 'seq'), axis=0, tiled=True)  55.7 us
  transfers between devices with their start and end apart: 19, of which 12 were waited for; matrix products, arithmetic and copies ran while one was open for 9% of the time, Pallas kernels for 0%

commit v1 on v0

--- a/solution.py
+++ b/solution.py
@@ -3,6 +3,8 @@
 import jax
 import jax.numpy as jnp
 from jax import lax
+from jax.experimental import pallas as pl
+from jax.experimental.pallas import tpu as pltpu
 from jax.sharding import PartitionSpec as P
 
 H = 16
@@ -437,6 +439,818 @@
     )
 
 
+MESH_ID = pl.DeviceIdType.MESH
+VMEM = pltpu.VMEM
+LINE = 4
+CHIPS = 8
+TOK = 128
+PAD = 128
+CHUNKS = 4
+ROWS = TOK // CHUNKS
+BF = jnp.bfloat16
+F32 = jnp.float32
+VSPEC = pl.BlockSpec(memory_space=pltpu.VMEM)
+
+
+def ring_of(chip):
+    z = chip // 2
+    x = chip % 2
+    return x * LINE + z + x * (LINE - 1 - 2 * z)
+
+
+def chip_of(ring):
+    x = ring // LINE
+    q = ring % LINE
+    return (q + x * (LINE - 1 - 2 * q)) * 2 + x
+
+
+class Place:
+    def __init__(self):
+        self.g = lax.axis_index("grp")
+        self.s = lax.axis_index("seq")
+        self.core = self.s % 2
+        self.chip = self.s // 2
+        self.x = self.chip % 2
+        self.ring = ring_of(self.chip)
+        self.step = 1 - 2 * self.core
+        self.next = {"seq": self.at(self.step) * 2 + self.core}
+        self.prev = {"seq": self.at(-self.step) * 2 + self.core}
+        self.sib = {"seq": self.s + 1 - 2 * self.core}
+        self.ynb = {"grp": 1 - self.g}
+        self.xnb = {"seq": self.s + 2 - 4 * self.x}
+
+    def at(self, offset):
+        return chip_of((self.ring + offset + 8 * CHIPS) % CHIPS)
+
+    def behind(self, t):
+        return self.at(-t * self.step)
+
+    def off(self, i):
+        return {"seq": ((self.chip + i + CHIPS) % CHIPS) * 2 + self.core}
+
+    def src(self, i):
+        return (self.chip - i + CHIPS) % CHIPS
+
+
+def greet(devices):
+    barrier = pltpu.get_barrier_semaphore()
+    for device in devices:
+        pl.semaphore_signal(barrier, inc=1, device_id=device, device_id_type=MESH_ID)
+    pl.semaphore_wait(barrier, len(devices))
+
+
+def remote(src, dst, send, recv, device):
+    return pltpu.make_async_remote_copy(
+        src_ref=src, dst_ref=dst, send_sem=send, recv_sem=recv, device_id=device,
+        device_id_type=MESH_ID,
+    )
+
+
+class RingGather:
+    sems = [pltpu.SemaphoreType.DMA((CHIPS, CHUNKS)), pltpu.SemaphoreType.DMA((CHIPS, CHUNKS))]
+
+    def __init__(self, place, all_ref, send, recv):
+        self.place, self.all, self.send, self.recv = place, all_ref, send, recv
+
+    def copy(self, t, k):
+        part = self.all.at[self.place.behind(t), pl.ds(k * ROWS, ROWS)]
+        return remote(part, part, self.send.at[t, k], self.recv.at[t, k], self.place.next)
+
+    def start(self, k=None):
+        for k in range(CHUNKS) if k is None else (k,):
+            self.copy(0, k).start()
+
+    def pump(self, t):
+        for k in range(CHUNKS):
+            self.copy(t - 1, k).wait_recv()
+            if t < CHIPS - 1:
+                self.copy(t, k).start()
+
+    def finish(self):
+        for t in range(CHIPS - 1):
+            for k in range(CHUNKS):
+                self.copy(t, k).wait_send()
+
+
+class RingScatter:
+    sems = [pltpu.SemaphoreType.DMA((CHIPS, CHUNKS)), pltpu.SemaphoreType.DMA((CHIPS, CHUNKS))]
+    bufs = [VMEM((CHIPS - 1, TOK, 1536), BF), VMEM((CHIPS - 1, TOK, 1536), BF)]
+
+    def __init__(self, place, out, held, send, recv):
+        self.place, self.out, self.held, self.send, self.recv = place, out, held, send, recv
+
+    def copy(self, t, k):
+        rows = pl.ds(k * ROWS, ROWS)
+        return remote(self.out.at[t, rows], self.held.at[t, rows], self.send.at[t, k],
+                      self.recv.at[t, k], self.place.next)
+
+    def dest(self, t):
+        return self.place.behind(t + 1)
+
+    def push(self, t, term):
+        for k in range(CHUNKS):
+            rows = pl.ds(k * ROWS, ROWS)
+            value = term(k)
+            if t > 0:
+                self.copy(t - 1, k).wait_recv()
+                value = value + self.held[t - 1, rows].astype(F32)
+            self.out[t, rows] = value.astype(BF)
+            self.copy(t, k).start()
+
+    def last(self, k):
+        self.copy(CHIPS - 2, k).wait_recv()
+        return self.held[CHIPS - 2, pl.ds(k * ROWS, ROWS)].astype(F32)
+
+    def finish(self):
+        for t in range(CHIPS - 1):
+            for k in range(CHUNKS):
+                self.copy(t, k).wait_send()
+
+
+class Spread:
+    sems = [pltpu.SemaphoreType.DMA((CHIPS,)), pltpu.SemaphoreType.DMA((CHIPS,)),
+            pltpu.SemaphoreType.DMA((CHIPS,)), pltpu.SemaphoreType.DMA((CHIPS,)),
+            pltpu.SemaphoreType.DMA((2 * CHIPS,)), pltpu.SemaphoreType.DMA((2 * CHIPS,))]
+
+    def __init__(self, place, slab, all_ref, local, *sems):
+        self.place, self.slab, self.all, self.local = place, slab, all_ref, local
+        self.s1, self.r1, self.s2, self.r2, self.s3, self.r3 = sems
+
+    def block(self, g, chip):
+        return self.all.at[g * 16 + chip * 2 + self.place.core]
+
+    def across(self, i):
+        p = self.place
+        return remote(self.slab.at[(p.chip + i) % CHIPS], self.block(p.g, p.chip), self.s1.at[i],
+                      self.r1.at[i], p.off(i))
+
+    def arrived(self, i):
+        p = self.place
+        return remote(self.slab.at[0], self.block(p.g, p.src(i)), self.s1.at[i], self.r1.at[i],
+                      p.off(i))
+
+    def to_y(self, i):
+        p = self.place
+        part = self.block(p.g, p.src(i))
+        return remote(part, part, self.s2.at[i], self.r2.at[i], p.ynb)
+
+    def from_y(self, i):
+        p = self.place
+        part = self.block(1 - p.g, p.src(i))
+        return remote(part, part, self.s2.at[i], self.r2.at[i], p.ynb)
+
+    def to_sib(self, i, other):
+        p = self.place
+        part = self.block((1 - p.g) if other else p.g, p.src(i))
+        n = i + CHIPS * other
+        return remote(part, part, self.s3.at[n], self.r3.at[n], p.sib)
+
+    def from_sib(self, i, other):
+        p = self.place
+        g = (1 - p.g) if other else p.g
+        part = self.all.at[g * 16 + p.src(i) * 2 + 1 - p.core]
+        n = i + CHIPS * other
+        return remote(part, part, self.s3.at[n], self.r3.at[n], p.sib)
+
+    def start(self):
+        p = self.place
+        own = pltpu.make_async_copy(self.slab.at[p.chip], self.block(p.g, p.chip), self.local)
+        own.start()
+        for i in range(1, CHIPS):
+            self.across(i).start()
+        own.wait()
+        self.to_y(0).start()
+        self.to_sib(0, 0).start()
+
+    def pump(self, i):
+        self.arrived(i).wait_recv()
+        self.to_y(i).start()
+        self.to_sib(i, 0).start()
+        self.from_y(i - 1).wait_recv()
+        self.to_sib(i - 1, 1).start()
+
+    def finish(self):
+        self.from_y(CHIPS - 1).wait_recv()
+        self.to_sib(CHIPS - 1, 1).start()
+        for i in range(CHIPS):
+            self.from_sib(i, 0).wait_recv()
+            self.from_sib(i, 1).wait_recv()
+        for i in range(CHIPS):
+            if i > 0:
+                self.across(i).wait_send()
+            self.to_y(i).wait_send()
+            self.to_sib(i, 0).wait_send()
+            self.to_sib(i, 1).wait_send()
+
+
+class Collect:
+    sems = [pltpu.SemaphoreType.DMA, pltpu.SemaphoreType.DMA, pltpu.SemaphoreType.DMA,
+            pltpu.SemaphoreType.DMA, pltpu.SemaphoreType.DMA((CHIPS,)),
+            pltpu.SemaphoreType.DMA((CHIPS,))]
+
+    @staticmethod
+    def bufs(rows, columns):
+        return [VMEM((16, rows, columns), BF), VMEM((16, rows, columns), BF),
+                VMEM((8, rows, columns), BF), VMEM((8, rows, columns), BF)]
+
+    def __init__(self, place, grads, got, bufs, sems):
+        self.place, self.grads, self.got = place, grads, got
+        self.sib_in, self.pair, self.y_in, self.total = bufs
+        self.s1, self.r1, self.s2, self.r2, self.s3, self.r3 = sems
+
+    def sib(self):
+        p = self.place
+        return remote(self.grads.at[:, 1 - p.core], self.sib_in, self.s1, self.r1, p.sib)
+
+    def y(self):
+        p = self.place
+        return remote(self.pair.at[pl.ds((1 - p.g) * 8, 8)], self.y_in, self.s2, self.r2, p.ynb)
+
+    def across(self, i):
+        p = self.place
+        return remote(self.total.at[(p.chip + i) % CHIPS], self.got.at[p.chip], self.s3.at[i],
+                      self.r3.at[i], p.off(i))
+
+    def arrived(self, i):
+        p = self.place
+        return remote(self.total.at[0], self.got.at[p.src(i)], self.s3.at[i], self.r3.at[i],
+                      p.off(i))
+
+    def start(self):
+        self.sib().start()
+
+    def mid(self):
+        p = self.place
+        self.sib().wait_recv()
+
+        def add(n, carry):
+            self.pair[n] = (self.grads[n, p.core].astype(F32) + self.sib_in[n].astype(F32)).astype(BF)
+            return carry
+
+        lax.fori_loop(0, 16, add, 0)
+        self.y().start()
+
+    def send(self):
+        p = self.place
+        self.y().wait_recv()
+
+        def add(n, carry):
+            self.total[n] = (self.pair[p.g * 8 + n].astype(F32) + self.y_in[n].astype(F32)).astype(BF)
+            return carry
+
+        lax.fori_loop(0, 8, add, 0)
+        for i in range(1, CHIPS):
+            self.across(i).start()
+        self.got[p.chip] = self.total[p.chip]
+
+    def finish(self):
+        for i in range(1, CHIPS):
+            self.arrived(i).wait_recv()
+        self.sib().wait_send()
+        self.y().wait_send()
+        for i in range(1, CHIPS):
+            self.across(i).wait_send()
+
+
+def dot(a, b):
+    return lax.dot_general(a, b, (((1,), (0,)), ((), ())), preferred_element_type=F32)
+
+
+def dot_nt(a, b):
+    return lax.dot_general(a, b, (((1,), (1,)), ((), ())), preferred_element_type=F32)
+
+
+def all_to_all_devices(place):
+    return [place.off(i) for i in range(1, CHIPS)]
+
+
+def call(body, outs, ins, scratch, collective_id, flops=0, nbytes=0):
+    kwargs = {}
+    if collective_id is not None:
+        kwargs = dict(collective_id=collective_id, has_side_effects=True)
+    return pl.pallas_call(
+        body,
+        out_shape=outs,
+        in_specs=[VSPEC] * len(ins),
+        out_specs=tuple(VSPEC for _ in outs) if isinstance(outs, (tuple, list)) else VSPEC,
+        scratch_shapes=scratch,
+        compiler_params=pltpu.CompilerParams(vmem_limit_bytes=60 << 20, **kwargs),
+        cost_estimate=pl.CostEstimate(flops=flops, bytes_accessed=nbytes, transcendentals=0),
+    )(*ins)
+
+
+def sds(*shape, dtype=BF):
+    return jax.ShapeDtypeStruct(shape, dtype)
+
+
+def rope(u, cosine, sine):
+    return u * cosine + pltpu.roll(u, 64, 1) * sine
+
+
+def whole(ref):
+    value = ref[...]
+    return value.reshape(value.shape[0] * value.shape[1], value.shape[2])
+
+
+def front_kernel(xh, slab, wo, cs, sn, xg, wqkv, wout, q, keys, values, wo2,
+                 ag_s, ag_r, s1, r1, s2, r2, s3, r3, ws, wr, ks, kr, vs, vr, local):
+    p = Place()
+    greet(all_to_all_devices(p) + [p.sib, p.ynb])
+    gather = RingGather(p, xg, ag_s, ag_r)
+    spread = Spread(p, slab, wqkv, local, s1, r1, s2, r2, s3, r3)
+    xg[p.chip] = xh[...]
+    gather.start()
+    wo2[p.g] = wo[...]
+    swap = remote(wo2.at[p.g], wo2.at[p.g], ws.at[0], wr.at[0], p.ynb)
+    swap.start()
+    spread.start()
+    gather.pump(1)
+    remote(wo2.at[1 - p.g], wo2.at[1 - p.g], ws.at[0], wr.at[0], p.ynb).wait_recv()
+    mine = p.x * 2 + p.core
+    theirs = (1 - p.x) * 2 + p.core
+    wout[mine] = wo2[p.x]
+    to_x = remote(wo2.at[1 - p.x], wout.at[mine], ws.at[1], wr.at[1], p.xnb)
+    to_x.start()
+    to_s = remote(wout.at[mine], wout.at[mine], ws.at[2], wr.at[2], p.sib)
+    to_s.start()
+    spread.pump(1)
+    gather.pump(2)
+    remote(wo2.at[0], wout.at[theirs], ws.at[1], wr.at[1], p.xnb).wait_recv()
+    to_s2 = remote(wout.at[theirs], wout.at[theirs], ws.at[3], wr.at[3], p.sib)
+    to_s2.start()
+    spread.pump(2)
+    for t in range(3, CHIPS):
+        gather.pump(t)
+        spread.pump(t)
+    spread.finish()
+
+    def kv_copy(i, n):
+        ref, send, recv = ((keys, ks, kr), (values, vs, vr))[n]
+        part = ref.at[2 * i + p.core]
+        return remote(part, part, send.at[i], recv.at[i], p.sib)
+
+    def kv_in(i, n):
+        ref, send, recv = ((keys, ks, kr), (values, vs, vr))[n]
+        part = ref.at[2 * i + 1 - p.core]
+        return remote(part, part, send.at[i], recv.at[i], p.sib)
+
+    def project(i, carry):
+        lin = dot(xg[i], whole(wqkv))
+        cosine, sine = cs[i], sn[i]
+        q[i, pl.ds(0, TOK)] = rope(lin[:, 0:128], cosine, sine).astype(BF)
+        q[i, pl.ds(TOK, TOK)] = rope(lin[:, 128:256], cosine, sine).astype(BF)
+        keys[2 * i + p.core] = rope(lin[:, 256:384], cosine, sine).astype(BF)
+        values[2 * i + p.core] = lin[:, 384:512].astype(BF)
+        kv_copy(i, 0).start()
+        kv_copy(i, 1).start()
+        return carry
+
+    lax.fori_loop(0, CHIPS, project, 0)
+    gather.finish()
+    swap.wait_send()
+    to_x.wait_send()
+    to_s.wait_send()
+    to_s2.wait_send()
+    rest = p.x * 2 + 1 - p.core
+    remote(wout.at[rest], wout.at[rest], ws.at[2], wr.at[2], p.sib).wait_recv()
+    rest2 = (1 - p.x) * 2 + 1 - p.core
+    remote(wout.at[rest2], wout.at[rest2], ws.at[3], wr.at[3], p.sib).wait_recv()
+    for i in range(CHIPS):
+        for n in range(2):
+            kv_copy(i, n).wait_send()
+            kv_in(i, n).wait_recv()
+
+
+def front(xh, slab, wo, cs, sn):
+    dma = pltpu.SemaphoreType.DMA
+    return call(
+        front_kernel,
+        (sds(CHIPS, TOK, 1536), sds(32, 48, 512), sds(4, 48, 1536), sds(CHIPS, 2 * TOK, PAD),
+         sds(2 * CHIPS, TOK, PAD), sds(2 * CHIPS, TOK, PAD), sds(2, 48, 1536)),
+        (xh, slab, wo, cs, sn),
+        RingGather.sems + Spread.sems + [dma((4,)), dma((4,))] + [dma((CHIPS,))] * 4 + [dma],
+        1, 2 * 1024 * 1536 * 512, 10 << 20,
+    )
+
+
+LOG2E = 1.4426950408889634
+SCALE = 1.0 / math.sqrt(96)
+SCALE2 = SCALE * LOG2E
+
+
+def scores_of(keys, query, limit, j):
+    s = dot_nt(keys[j], query) * SCALE2
+    pos = lax.broadcasted_iota(jnp.int32, s.shape, 0) + j * 256
+    return jnp.where(pos.astype(F32) <= limit, s, neg_big)
+
+
+def attn_kernel(q, keys, values, limits, bg, slab, wd, mix, mix_t, stat, bgg, wgu, wdown,
+                vt, ag_s, ag_r, s1, r1, s2, r2, s3, r3, ws, wr, local):
+    p = Place()
+    greet(all_to_all_devices(p) + [p.sib, p.ynb])
+    gather = RingGather(p, bgg, ag_s, ag_r)
+    spread = Spread(p, slab, wgu, local, s1, r1, s2, r2, s3, r3)
+    bgg[p.chip] = bg[...]
+    gather.start()
+    spread.start()
+    here = p.g * 2 + p.core
+    there = (1 - p.g) * 2 + p.core
+    wdown[here] = wd[...]
+    swap = remote(wdown.at[here], wdown.at[here], ws.at[0], wr.at[0], p.ynb)
+    swap.start()
+    to_s = remote(wdown.at[here], wdown.at[here], ws.at[1], wr.at[1], p.sib)
+    to_s.start()
+    to_s2 = remote(wdown.at[there], wdown.at[there], ws.at[2], wr.at[2], p.sib)
+
+    def turn(n, carry):
+        vt[n] = values[n].astype(F32).T.astype(BF)
+        return carry
+
+    lax.fori_loop(0, CHIPS, turn, 0)
+
+    def attend(i):
+        query = q[i]
+        limit = limits[i]
+
+        def chunk(j, state):
+            top, total, acc = state
+            s = scores_of(keys, query, limit, j)
+            new_top = jnp.maximum(top, jnp.max(s, axis=0, keepdims=True))
+            fade = jnp.exp2(top - new_top)
+            w = jnp.exp2(s - new_top)
+            total = total * fade + jnp.sum(w, axis=0, keepdims=True)
+            acc = acc * fade + dot(vt[j], w.astype(BF))
+            return new_top, total, acc
+
+        start = (jnp.full((1, 256), neg_big, F32), jnp.zeros((1, 256), F32),
+                 jnp.zeros((PAD, 256), F32))
+        top, total, acc = lax.fori_loop(0, i + 1, chunk, start)
+        acc = acc / total
+        mix_t[i] = acc
+        stat[i] = top + jnp.log2(total)
+        out = acc.T.astype(BF)
+        mix[i, :, pl.ds(0, PAD)] = out[:TOK]
+        mix[i, :, pl.ds(PAD, PAD)] = out[TOK:]
+
+    for i in range(CHIPS):
+        attend(i)
+        if i > 0:
+            gather.pump(i)
+            spread.pump(i)
+        if i == 3:
+            remote(wdown.at[there], wdown.at[there], ws.at[0], wr.at[0], p.ynb).wait_recv()
+            to_s2.start()
+    spread.finish()
+    gather.finish()
+    swap.wait_send()
+    to_s.wait_send()
+    to_s2.wait_send()
+    rest = p.g * 2 + 1 - p.core
+    remote(wdown.at[rest], wdown.at[rest], ws.at[1], wr.at[1], p.sib).wait_recv()
+    rest2 = (1 - p.g) * 2 + 1 - p.core
+    remote(wdown.at[rest2], wdown.at[rest2], ws.at[2], wr.at[2], p.sib).wait_recv()
+
+
+def attend_all(q, keys, values, limits, bg, slab, wd):
+    dma = pltpu.SemaphoreType.DMA
+    return call(
+        attn_kernel,
+        (sds(CHIPS, TOK, 2 * PAD), sds(CHIPS, PAD, 256, dtype=F32), sds(CHIPS, 1, 256, dtype=F32),
+         sds(CHIPS, TOK, 1536), sds(32, 48, 1024), sds(4, 128, 1536)),
+        (q, keys, values, limits, bg, slab, wd),
+        [VMEM((CHIPS, PAD, 256), BF)] + RingGather.sems + Spread.sems
+        + [dma((3,)), dma((3,)), dma],
+        2, 2 * 1024 * 2048 * 256, 10 << 20,
+    )
+
+
+def mid_kernel(mix, wout, tokens, hidden, scale, xg, part, out, held, rs_s, rs_r, ag_s, ag_r):
+    p = Place()
+    greet([p.next, p.prev])
+    scatter = RingScatter(p, out, held, rs_s, rs_r)
+    gather = RingGather(p, xg, ag_s, ag_r)
+    for t in range(CHIPS):
+        part[...] = dot(mix[scatter.dest(t)], wout[...])
+        if t < CHIPS - 1:
+            scatter.push(t, lambda k: part[pl.ds(k * ROWS, ROWS)])
+    for k in range(CHUNKS):
+        rows = pl.ds(k * ROWS, ROWS)
+        h = tokens[rows] + part[rows] + scatter.last(k)
+        r = lax.rsqrt(jnp.mean(h * h, axis=-1, keepdims=True) + epsilon)
+        hidden[rows] = h
+        scale[rows] = jnp.broadcast_to(r, (ROWS, 128))
+        xg[p.chip, rows] = (h * r).astype(BF)
+        gather.start(k)
+    for t in range(1, CHIPS):
+        gather.pump(t)
+    scatter.finish()
+    gather.finish()
+
+
+def middle(mix, wout, tokens):
+    return call(
+        mid_kernel,
+        (sds(TOK, 1536, dtype=F32), sds(TOK, 128, dtype=F32), sds(CHIPS, TOK, 1536)),
+        (mix, wout, tokens),
+        [VMEM((TOK, 1536), F32)] + RingScatter.bufs + RingScatter.sems + RingGather.sems,
+        3, 2 * 1024 * 256 * 1536, 10 << 20,
+    )
+
+
+def back_kernel(gub, wgu, hidden, scale, bg, grad, low_all, part, out, held, rs_s, rs_r, ag_s, ag_r):
+    p = Place()
+    greet([p.next, p.prev])
+    scatter = RingScatter(p, out, held, rs_s, rs_r)
+    gather = RingGather(p, low_all, ag_s, ag_r)
+    for t in range(CHIPS):
+        part[...] = dot_nt(gub[scatter.dest(t)], wgu[...])
+        if t < CHIPS - 1:
+            scatter.push(t, lambda k: part[pl.ds(k * ROWS, ROWS)])
+    for k in range(CHUNKS):
+        rows = pl.ds(k * ROWS, ROWS)
+        a = part[rows] + scatter.last(k)
+        h = hidden[rows]
+        r = scale[rows, pl.ds(0, 1)]
+        value = bg[rows].astype(F32) + r * a - h * (r * r * r) * jnp.mean(a * h, axis=-1, keepdims=True)
+        grad[rows] = value
+        low_all[p.chip, rows] = value.astype(BF)
+        gather.start(k)
+    for t in range(1, CHIPS):
+        gather.pump(t)
+    scatter.finish()
+    gather.finish()
+
+
+def back(gub, wgu, hidden, scale, bg):
+    return call(
+        back_kernel,
+        (sds(TOK, 1536, dtype=F32), sds(CHIPS, TOK, 1536)),
+        (gub, wgu, hidden, scale, bg),
+        [VMEM((TOK, 1536), F32)] + RingScatter.bufs + RingScatter.sems + RingGather.sems,
+        4, 2 * 1024 * 1024 * 1536, 10 << 20,
+    )
+
+
+def attn_back_kernel(q, keys, values, limits, grad_t, grad, mix_t, stat, cs, sn, branch, dgu, dwd,
+                     back_out, branch_sum, got, dwd_sum,
+                     kt, dk, dv, dkv_low, dkv_in, out, held, sib_in, pair, y_in, total,
+                     d_in, d_pair, d_y,
+                     rs_s, rs_r, c1, c2, c3, c4, c5, c6, ds, dr, xs, xr):
+    p = Place()
+    greet(all_to_all_devices(p) + [p.sib, p.ynb])
+    scatter = RingScatter(p, out, held, rs_s, rs_r)
+    collect = Collect(p, dgu, got, (sib_in, pair, y_in, total), (c1, c2, c3, c4, c5, c6))
+    collect.start()
+    fold = remote(dwd.at[:, 1 - p.core], d_in, ds.at[0], dr.at[0], p.sib)
+    fold.start()
+    scatter.push(0, lambda k: branch[scatter.dest(0), pl.ds(k * ROWS, ROWS)].astype(F32))
+
+    def turn(n, carry):
+        kt[n] = keys[n].astype(F32).T.astype(BF)
+        dk[n] = jnp.zeros((256, PAD), F32)
+        dv[n] = jnp.zeros((256, PAD), F32)
+        return carry
+
+    lax.fori_loop(0, CHIPS, turn, 0)
+
+    def attend(i):
+        query = q[i]
+        limit = limits[i]
+        do = grad[i]
+        lse = stat[i]
+        delta = jnp.sum(grad_t[i].astype(F32) * mix_t[i], axis=0, keepdims=True)
+
+        def chunk(j, acc):
+            w = jnp.exp2(scores_of(keys, query, limit, j) - lse)
+            dp = dot_nt(values[j], do)
+            ds_low = (w * (dp - delta)).astype(BF)
+            dk[j] += dot(ds_low, query)
+            dv[j] += dot(w.astype(BF), do)
+            return acc + dot(kt[j], ds_low)
+
+        acc = lax.fori_loop(0, i + 1, chunk, jnp.zeros((PAD, 256), F32))
+        dq = acc.T * SCALE
+        cosine, sine = cs[i], -sn[i]
+        back_out[i, :, pl.ds(0, PAD)] = rope(dq[:TOK], cosine, sine).astype(BF)
+        back_out[i, :, pl.ds(PAD, PAD)] = rope(dq[TOK:], cosine, sine).astype(BF)
+
+    y_fold = remote(d_pair.at[1 - p.g], d_y, ds.at[1], dr.at[1], p.ynb)
+    for i in range(CHIPS):
+        attend(i)
+        if 0 < i < CHIPS - 1:
+            scatter.push(i, lambda k: branch[scatter.dest(i), pl.ds(k * ROWS, ROWS)].astype(F32))
+        if i == 1:
+            fold.wait_recv()
+            for n in range(2):
+                d_pair[n] = (dwd[n, p.core].astype(F32) + d_in[n].astype(F32)).astype(BF)
+            y_fold.start()
+            collect.mid()
+        if i == 3:
+            collect.send()
+    for n in range(CHIPS):
+        for c in range(2):
+            rows = pl.ds(c * TOK, TOK)
+            dkv_low[0, n, c] = dk[n, rows].astype(BF)
+            dkv_low[1, n, c] = dv[n, rows].astype(BF)
+    swap = remote(dkv_low.at[:, :, 1 - p.core], dkv_in, xs, xr, p.sib)
+    swap.start()
+    for k in range(CHUNKS):
+        rows = pl.ds(k * ROWS, ROWS)
+        branch_sum[rows] = branch[p.chip, rows].astype(F32) + scatter.last(k)
+    y_fold.wait_recv()
+    dwd_sum[...] = d_pair[p.g].astype(F32) + d_y[...].astype(F32)
+    swap.wait_recv()
+
+    def keys_back(n, carry):
+        own = pl.ds(pl.multiple_of(p.core * TOK, TOK), TOK)
+        back_out[n, :, pl.ds(2 * PAD, PAD)] = rope(
+            (dk[n, own] + dkv_in[0, n].astype(F32)) * SCALE, cs[n], -sn[n]).astype(BF)
+        back_out[n, :, pl.ds(3 * PAD, PAD)] = (dv[n, own] + dkv_in[1, n].astype(F32)).astype(BF)
+        return carry
+
+    lax.fori_loop(0, CHIPS, keys_back, 0)
+    collect.finish()
+    scatter.finish()
+    fold.wait_send()
+    y_fold.wait_send()
+    swap.wait_send()
+
+
+def attend_back(q, keys, values, limits, grad_t, grad, mix_t, stat, cs, sn, branch, dgu, dwd):
+    dma = pltpu.SemaphoreType.DMA
+    return call(
+        attn_back_kernel,
+        (sds(CHIPS, TOK, 4 * PAD), sds(TOK, 1536, dtype=F32), sds(CHIPS, 48, 1024),
+         sds(TOK, 1536, dtype=F32)),
+        (q, keys, values, limits, grad_t, grad, mix_t, stat, cs, sn, branch, dgu, dwd),
+        [VMEM((CHIPS, PAD, 256), BF), VMEM((CHIPS, 256, PAD), F32), VMEM((CHIPS, 256, PAD), F32),
+         VMEM((2, CHIPS, 2, TOK, PAD), BF), VMEM((2, CHIPS, TOK, PAD), BF)]
+        + RingScatter.bufs + Collect.bufs(48, 1024)
+        + [VMEM((2, TOK, 1536), BF), VMEM((2, TOK, 1536), BF), VMEM((TOK, 1536), BF)]
+        + RingScatter.sems + Collect.sems + [dma((2,)), dma((2,)), dma, dma],
+        5, 5 * 1024 * 2048 * 256, 20 << 20,
+    )
+
+
+def last_kernel(grads, wqkv, dqkv, dout, csum, got, dout_sum,
+                part, out, held, sib_in, pair, y_in, total, o_in, o_pair, o_two, o_y,
+                rs_s, rs_r, c1, c2, c3, c4, c5, c6, os, orr):
+    p = Place()
+    greet(all_to_all_devices(p) + [p.sib, p.ynb])
+    scatter = RingScatter(p, out, held, rs_s, rs_r)
+    collect = Collect(p, dqkv, got, (sib_in, pair, y_in, total), (c1, c2, c3, c4, c5, c6))
+    collect.start()
+    fold = remote(dout.at[:, 1 - p.core], o_in, os.at[0], orr.at[0], p.sib)
+    fold.start()
+    x_fold = remote(o_pair.at[1 - p.x], o_two.at[p.x], os.at[1], orr.at[1], p.xnb)
+    x_here = remote(o_pair.at[0], o_two.at[1 - p.x], os.at[1], orr.at[1], p.xnb)
+    y_fold = remote(o_two.at[1 - p.g], o_y, os.at[2], orr.at[2], p.ynb)
+    for t in range(CHIPS):
+        part[...] = dot_nt(grads[scatter.dest(t)], whole(wqkv))
+        if t < CHIPS - 1:
+            scatter.push(t, lambda k: part[pl.ds(k * ROWS, ROWS)])
+        if t == 0:
+            fold.wait_recv()
+            for n in range(2):
+                o_pair[n] = (dout[n, p.core].astype(F32) + o_in[n].astype(F32)).astype(BF)
+            x_fold.start()
+            collect.mid()
+        if t == 1:
+            o_two[p.x] = o_pair[p.x]
+            x_here.wait_recv()
+            y_fold.start()
+        if t == 2:
+            collect.send()
+    for k in range(CHUNKS):
+        rows = pl.ds(k * ROWS, ROWS)
+        csum[rows] = part[rows] + scatter.last(k)
+    y_fold.wait_recv()
+    dout_sum[...] = o_two[p.g].astype(F32) + o_y[...].astype(F32)
+    collect.finish()
+    scatter.finish()
+    fold.wait_send()
+    x_fold.wait_send()
+    y_fold.wait_send()
+
+
+def last(grads, wqkv, dqkv, dout):
+    dma = pltpu.SemaphoreType.DMA
+    return call(
+        last_kernel,
+        (sds(TOK, 1536, dtype=F32), sds(CHIPS, 48, 512), sds(48, 1536, dtype=F32)),
+        (grads, wqkv, dqkv, dout),
+        [VMEM((TOK, 1536), F32)] + RingScatter.bufs + Collect.bufs(48, 512)
+        + [VMEM((2, 48, 1536), BF), VMEM((2, 48, 1536), BF), VMEM((2, 48, 1536), BF), VMEM((48, 1536), BF)]
+        + RingScatter.sems + Collect.sems + [dma((3,)), dma((3,))],
+        6, 2 * 1024 * 512 * 1536, 10 << 20,
+    )
+
+
+def pad_heads(weight, heads):
+    w = weight.reshape(weight.shape[0], heads, 2, 48)
+    return jnp.pad(w, ((0, 0), (0, 0), (0, 0), (0, 16))).reshape(weight.shape[0], heads, PAD)
+
+
+def by_chip(slab):
+    return slab.reshape((2, LINE) + slab.shape[1:]).swapaxes(0, 1).reshape(slab.shape)
+
+
+def by_head(slab):
+    return slab.reshape((LINE, 2) + slab.shape[1:]).swapaxes(0, 1).reshape(slab.shape)
+
+
+def plane_device(hidden_in, lengths, attn_gain, w_query, w_key, w_value, w_out, mlp_gain, w_gate, w_up,
+                 w_down, out_grad):
+    core = lax.axis_index("seq") % 2
+    length = lengths[0]
+    gain_one = attn_gain.astype(F32)[:, None]
+    gain_two = mlp_gain.astype(F32)[:, None]
+    tokens = hidden_in[0].astype(F32)
+    r_one = norm_scale(tokens)
+    xh = (tokens * r_one).astype(BF)
+    own_pos = lax.axis_index("seq") * TOK + jnp.arange(TOK, dtype=jnp.int32)
+    valid = (own_pos < length).astype(F32)[:, None]
+    bg = (valid * out_grad[0].astype(F32)).astype(BF)
+
+    scaled = lambda w, gain: (w.astype(F32) * gain).astype(BF)
+    wq = pad_heads(scaled(w_query, gain_one), 16).reshape(48, 8, 2 * PAD)
+    wk = pad_heads(scaled(w_key, gain_one), 8)
+    wv = pad_heads(scaled(w_value, gain_one), 8)
+    slab_qkv = by_chip(jnp.concatenate([wq, wk, wv], axis=-1).swapaxes(0, 1))
+    ff = lambda w: scaled(w, gain_two).reshape(48, 2, 8, 256).transpose(2, 0, 1, 3).reshape(8, 48, 512)
+    slab_gu = jnp.concatenate([ff(w_gate), ff(w_up)], axis=-1)
+
+    positions = (2 * jnp.arange(CHIPS, dtype=jnp.int32)[:, None] + core) * TOK + jnp.arange(TOK, dtype=jnp.int32)
+    cosine, sine = rope_tables(positions.reshape(-1))
+    cosine = jnp.pad(cosine, ((0, 0), (0, 16)))
+    sine = jnp.pad(sine, ((0, 0), (0, 16)))
+    cs = jnp.concatenate([cosine, cosine], axis=-1).reshape(CHIPS, TOK, PAD)
+    sn = jnp.concatenate([-sine, sine], axis=-1).reshape(CHIPS, TOK, PAD)
+    limit = jnp.minimum(positions, length - 1).astype(F32)
+    limits = jnp.concatenate([limit, limit], axis=-1).reshape(CHIPS, 1, 2 * TOK)
+
+    xg, wqkv, wout4, q, keys, values, unused = front(xh, slab_qkv, w_out, cs, sn)
+    keys = keys.reshape(CHIPS, 256, PAD)
+    values = values.reshape(CHIPS, 256, PAD)
+    mix, mix_t, stat, bgg, wgu, wdown = attend_all(q, keys, values, limits, bg, slab_gu, w_down)
+    wout = jnp.pad(wout4, ((0, 0), (0, 16), (0, 0))).reshape(256, 1536)
+    wgu = wgu.reshape(1536, 1024)
+    wdown = wdown.reshape(512, 1536)
+    hidden, scale, x2 = middle(mix, wout, tokens)
+
+    x2f = x2.reshape(1024, 1536)
+    bgf = bgg.reshape(1024, 1536)
+    lin = jnp.dot(x2f, wgu, preferred_element_type=F32)
+    gate_lin, up_lin = lin[:, :512], lin[:, 512:]
+    sigma = jax.nn.sigmoid(gate_lin)
+    silu_act = gate_lin * sigma
+    inner = (silu_act * up_lin).astype(BF)
+    inner_grad = jnp.einsum("td,fd->tf", bgf, wdown, preferred_element_type=F32)
+    gate_back = (inner_grad * up_lin * (sigma + gate_lin * sigma * (1.0 - sigma))).astype(BF)
+    up_back = (inner_grad * silu_act).astype(BF)
+    gub = jnp.concatenate([gate_back, up_back], axis=-1)
+    grad, mix_back = back(gub.reshape(CHIPS, TOK, 1024), wgu, hidden, scale, bg)
+    branch = jnp.dot(inner, wdown, preferred_element_type=F32).astype(BF).reshape(CHIPS, TOK, 1536)
+    dgu = jnp.einsum("td,tf->df", x2f, gub, preferred_element_type=F32).astype(BF)
+    dwd = jnp.einsum("tf,td->fd", inner, bgf, preferred_element_type=F32).astype(BF)
+
+    mixb = mix_back.reshape(1024, 1536)
+    attn_back = jnp.einsum("te,de->td", mixb, wout, preferred_element_type=F32).astype(BF)
+    dout = jnp.einsum("td,te->de", mix.reshape(1024, 256), mixb, preferred_element_type=F32).astype(BF)
+    dout = dout.reshape(2, 2, 64, 1536)[:, :, :48]
+    grad_rows = attn_back.reshape(CHIPS, TOK, 2, PAD).swapaxes(1, 2).reshape(CHIPS, 2 * TOK, PAD)
+    grads, branch_sum, got_gu, dwd_sum = attend_back(
+        q, keys, values, limits, grad_rows.swapaxes(1, 2), grad_rows, mix_t, stat, cs, sn, branch,
+        dgu.reshape(16, 2, 48, 1024), dwd.reshape(2, 2, TOK, 1536))
+    result = (valid * (hidden + branch_sum)).astype(BF)[None]
+    dqkv = jnp.einsum("td,te->de", xg.reshape(1024, 1536), grads.reshape(1024, 512),
+                      preferred_element_type=F32).astype(BF)
+    csum, got_qkv, dout_sum = last(grads, wqkv, dqkv.reshape(16, 2, 48, 512), dout)
+    input_back = grad + r_one * csum - tokens * (r_one * r_one * r_one) * jnp.mean(
+        csum * tokens, axis=-1, keepdims=True)
+
+    got_gu = got_gu.astype(F32)
+    unff = lambda v: v.reshape(8, 48, 2, 256).transpose(1, 2, 0, 3).reshape(48, 4096)
+    d_gate, d_up = unff(got_gu[:, :, :512]), unff(got_gu[:, :, 512:])
+    got_qkv = by_head(got_qkv).swapaxes(0, 1).astype(F32)
+    unpad = lambda v: v.reshape(48, -1, 2, 64)[:, :, :, :48].reshape(48, -1)
+    d_q, d_k, d_v = unpad(got_qkv[:, :, :256]), unpad(got_qkv[:, :, 256:384]), unpad(got_qkv[:, :, 384:])
+    along = lambda w, d: jnp.sum(w.astype(F32) * d, axis=-1)
+    return (
+        result,
+        input_back.astype(BF)[None],
+        along(w_query, d_q) + along(w_key, d_k) + along(w_value, d_v),
+        d_q * gain_one,
+        d_k * gain_one,
+        d_v * gain_one,
+        dout_sum,
+        along(w_gate, d_gate) + along(w_up, d_up),
+        d_gate * gain_two,
+        d_up * gain_two,
+        dwd_sum,
+    )
+
+
 def solution(mesh):
     placed = (
         P("grp", "seq", None),
@@ -452,8 +1266,9 @@
         P(("grp", "seq"), None),
         P("grp", "seq", None),
     )
+    small = mesh.shape["grp"] == 2 and mesh.shape["seq"] == 2 * CHIPS
     return jax.shard_map(
-        per_device,
+        plane_device if small else per_device,
         mesh=mesh,
         in_specs=placed,
         out_specs=(

time: 1960 us -> 466 us (0.24)
  waiting for transfers between devices: 1470 us -> 0 us
  Pallas kernels: 0 us -> 380 us
  local copies, waits for them, and re-layouts: 134 us -> 20.4 us
  blocking collectives: 107 us -> 0 us
  matrix products: 121 us -> 34.1 us
  loops' own time: 63.5 us -> 0 us
    unnamed x22 -> x0, waiting for transfers between devices: 1010 us -> none
    all_gather x9 -> x0, waiting for transfers between devices: 456 us -> none  [the longest x1 89.4 us: per_device(): lax.all_gather(w_up, ('grp', 'seq'), axis=0, tiled=True)]
    pallas_call x0 -> x6, Pallas kernels: none -> 380 us  [call(): pl.pallas_call(body, out_shape=outs, in_specs=[VSPEC] * len(ins), out_spe...]
    unnamed x3 -> x0, blocking collectives: 107 us -> none
    dot_general x30 -> x8, matrix products: 121 us -> 34.1 us  [the longest x1 6.62 us: plane_device(): lin = jnp.dot(x2f, wgu, preferred_element_type=F32)]
    another operation x27 -> x0, loops' own time: 63.5 us -> none  [the longest x1 21.2 us: attend_forward(): lax.scan(value_step, (start_acc, start_acc), (key_blocks, value_blocks, o...]
    unnamed x96 -> x48, local copies, waits for them, and re-layouts: 56.6 us -> 2.76 us
    dynamic_slice x24 -> x0, local copies, waits for them, and re-layouts: 19.7 us -> none  [attend_forward(): lax.scan(stat_step, (start_max, start_total), (key_blocks, offsets))]
  transfers between devices with their start and end apart: 19 -> 0, of which waited for: 12 -> 0; matrix products, arithmetic and copies ran while one was open for 9% -> 0% of each run, Pallas kernels for 0% -> 0%
where the time goes in v1:
time: 466 us; the launch traced here: 457 us
  Pallas kernels  380 us (82%)
  matrix products  34.1 us (7%)
  other arithmetic  20.7 us (4%)
  local copies, waits for them, and re-layouts  20.4 us (4%)
    pallas_call x6, Pallas kernels, call(): pl.pallas_call(body, out_shape=outs, in_specs=[VSPEC] * len(ins), out_spe...  380 us

profile of v1, /device:TPU:0, one launch (start us, length us, event | category | flops | bytes accessed | tf_op | source)
XLA Modules:
  0.0 457.4 jit_solution(9053979472972952228)
XLA Ops:
  1.3 0.7 convert_element_type.144
  2.0 0.7 convert_element_type.157
  2.6 1.2 fusion.7
  3.9 0.6 reshape.221.limits
  4.5 1.0 fusion.15
  5.5 1.0 fusion.17
  9.0 0.8 copy.48
  9.8 0.9 fusion.6.bg
  10.7 0.9 fusion.8.xh
  11.5 1.0 bitcast_convert_fusion.tokens
  14.0 1.0 pad_maximum_fusion.1.slab
  15.0 1.9 multiply_sine_fusion
  16.9 1.0 pad_maximum_fusion.2
  18.0 1.0 pad_maximum_fusion.3
  19.0 59.2 %shard_map.203 = (bf16[8,128,1536]{2,1,0:T(8,128)(2,1)}, bf16[32,48,512]{2,1,0:T(8,128)(2,1)}, bf16[4,48,1536]{2,1,0:T(8,128)(2,1)}, bf16[8,256,128]{2,1,0:T(8,1...) custom-call(bf16[128,1536]{1,0:T(8,128)(2,1)} %fusion.8.xh, ...), custom_call_target="tpu_custom_call" | custom-call | flops 1610612736 | bytes 10485760 | tf_op jit(solution)/shard_map/pallas_call | solution.py:731
  78.2 2.0 pad.27
  80.2 64.2 %shard_map.204 = (bf16[8,128,256]{2,1,0:T(8,128)(2,1)}, f32[8,128,256]{2,1,0:T(8,128)}, f32[8,1,256]{2,1,0:T(1,128)}, bf16[8,128,1536]{2,1,0:T(8,128)(2,1)}, bf1...) custom-call(bf16[8,256,128]{2,1,0:T(8,128)(2,1)} %get-tuple-element.35.q, bf16[8,256,128]{2,1,0:T(8,128)(2,1)} %bitcast.133, ...), custom_call_target="tpu_custom_call" | custom-call | flops 1073741824 | bytes 10485760 | tf_op jit(solution)/shard_map/pallas_call | solution.py:731
  144.4 67.5 %shard_map.205 = (f32[128,1536]{1,0:T(8,128)}, f32[128,128]{1,0:T(8,128)}, bf16[8,128,1536]{2,1,0:T(8,128)(2,1)}) custom-call(bf16[8,128,256]{2,1,0:T(8,128)(2,1)} %get-tuple-element.38.mix, bf16[256,1536]{1,0:T(8,128)(2,1)} %bitcast.131, f32[128,1536]{1,0:T(8,128)} %bitcast_convert_fusion.tokens), custom_call_target="tpu_custom_call" | custom-call | flops 805306368 | bytes 10485760 | tf_op jit(solution)/shard_map/pallas_call | solution.py:731
  211.9 6.6 %fusion.23 = f32[1024,1024]{0,1:T(8,128)S(1)} fusion(bf16[1024,1536]{1,0:T(8,128)(2,1)} %bitcast.144, bf16[1536,1024]{1,0:T(8,128)(2,1)} %bitcast.140), kind=kOutput, calls=%fused_computation.77 | convolution fusion | flops 3221225472 | bytes 10485760 | tf_op jit(solution)/shard_map/dot_general | solution.py:1203
  218.6 2.4 multiply_convert_fusion.2
  221.1 3.0 convolution_convert_fusion.2
  224.0 6.0 %convolution_convert_fusion.1 = bf16[1536,1024]{1,0:T(8,128)(2,1)} fusion(bf16[1024,1536]{1,0:T(8,128)(2,1)S(1)} %bitcast.145, bf16[1024,512]{0,1:T(8,128)(2,1)S(1)} %get-tuple-element.60, bf16[1024,512]{0,1:T(8,128)(2,1)S(1)} %get-tuple-element.59), kind=kOutput, calls=%fused_computation.1 | convolution fusion | flops 3226992640 | bytes 8388608 | tf_op jit(solution)/shard_map/td,tf->df/dot_general | solution.py:1214
  230.2 2.8 copy.51
  233.0 69.7 %shard_map.206 = (f32[128,1536]{1,0:T(8,128)}, bf16[8,128,1536]{2,1,0:T(8,128)(2,1)}) custom-call(bf16[8,128,1024]{2,1,0:T(8,128)(2,1)} %bitcast.120, bf16[1536,1024]{1,0:T(8,128)(2,1)} %bitcast.141, f32[128,1536]{1,0:T(8,128)} %get-tuple-element.40.hidden, f32[128,128]{1,0:T(8,128)} %get-tuple-element.45.scale, bf16[128,1536]{1,0:T(8,128)(2,1)} %fusion.6.bg), custom_call_target="tpu_custom_call" | custom-call | flops 3221225472 | bytes 10485760 | tf_op jit(solution)/shard_map/pallas_call | solution.py:731
  302.7 2.9 convolution_convert_fusion.3
  305.9 3.3 fusion.1
  309.1 0.9 slice.46.dout
  310.0 1.0 copy.53.grad_t
  311.0 4.8 %convolution_convert_fusion = bf16[1024,1536]{1,0:T(8,128)(2,1)} fusion(bf16[1024,512]{0,1:T(8,128)(2,1)} %copy-done.20, bf16[512,1536]{1,0:T(8,128)(2,1)S(1)} %bitcast.148), kind=kOutput, calls=%fused_computation | convolution fusion | flops 1612185600 | bytes 5767168 | tf_op jit(solution)/shard_map/dot_general | solution.py:1213
  315.8 70.5 %shard_map.207 = (bf16[8,128,512]{2,1,0:T(8,128)(2,1)}, f32[128,1536]{1,0:T(8,128)}, bf16[8,48,1024]{2,1,0:T(8,128)(2,1)}, f32[128,1536]{1,0:T(8,128)}) custom-call(bf16[8,256,128]{2,1,0:T(8,128)(2,1)} %get-tuple-element.35.q, bf16[8,256,128]{2,1,0:T(8,128)(2,1)} %bitcast.134, bf16[8,256,128]{2,1,0:T(8,128)(2,1)} %bitcast.136, ...), custom_call_target="tpu_custom_call" | custom-call | flops 2684354560 | bytes 20971520 | tf_op jit(solution)/shard_map/pallas_call | solution.py:731
  386.3 5.2 %fusion = bf16[1536,512]{1,0:T(8,128)(2,1)} fusion(bf16[8,128,1536]{2,1,0:T(8,128)(2,1)} %get-tuple-element.53, bf16[8,128,512]{2,1,0:T(8,128)(2,1)} %get-tuple-element.51.grads), kind=kOutput, calls=%fused_computation.3 | convolution fusion | flops 1611399168 | bytes 5767168 | tf_op jit(solution)/shard_map/td,te->de/dot_general | solution.py:1226
  391.4 48.8 %shard_map.208 = (f32[128,1536]{1,0:T(8,128)}, bf16[8,48,512]{2,1,0:T(8,128)(2,1)}, f32[48,1536]{1,0:T(8,128)}) custom-call(bf16[8,128,512]{2,1,0:T(8,128)(2,1)} %get-tuple-element.51.grads, bf16[32,48,512]{2,1,0:T(8,128)(2,1)} %get-tuple-element.52.wqkv, bf16[16,2,48,512]{3,2,1,0:T(8,128)(2,1)} %bitcast.149, bf16[2,2,48,1536]{3,2,1,0:T(8,128)(2,1)} %slice.46.dout), custom_call_target="tpu_custom_call" | custom-call | flops 1610612736 | bytes 10485760 | tf_op jit(solution)/shard_map/pallas_call | solution.py:731
  440.2 1.3 fusion.12
  441.6 2.3 fusion.13
  444.7 0.5 reshape.243
  445.3 0.5 reshape.240
  445.7 1.1 reshape.241
  446.8 0.9 broadcast_multiply_fusion.2
  448.1 0.5 reshape.245
  448.7 0.9 broadcast_multiply_fusion.3
  449.6 0.5 add_add_fusion
  450.4 0.5 reshape.248
  450.9 0.5 copy.61
  451.8 0.5 reshape.246
  453.3 1.5 broadcast_multiply_fusion
  454.8 0.5 add.108
  455.3 0.7 copy.75
  456.0 0.9 copy.76
  (84 shorter events, 7.2 us)
Async XLA Ops:
  6.5 3.2 copy-start.11
  7.0 3.7 copy-start
  8.1 4.4 copy-start.3
  8.1 4.4 copy-start.4
  211.9 6.7 %copy-start.16 = (bf16[8,128,1536]{2,1,0:T(8,128)(2,1)S(1)}, bf16[8,128,1536]{2,1,0:T(8,128)(2,1)}, u32[]{:S(2)}) copy-start(bf16[8,128,1536]{2,1,0:T(8,128)(2,1)} %get-tuple-element.41) | copy-start | bytes 9437188
  211.9 6.7 %copy-start.18 = (bf16[4,128,1536]{2,1,0:T(8,128)(2,1)S(1)}, bf16[4,128,1536]{2,1,0:T(8,128)(2,1)}, u32[]{:S(2)}) copy-start(bf16[4,128,1536]{2,1,0:T(8,128)(2,1)} %get-tuple-element.42) | copy-start | bytes 4718596
  221.0 3.0 copy-start.20
  221.1 3.0 copy-start.17
  233.0 69.7 %copy-start.6 = (bf16[4,64,1536]{2,1,0:T(8,128)(2,1)S(1)}, bf16[4,64,1536]{2,1,0:T(8,128)(2,1)}, u32[]{:S(2)}) copy-start(bf16[4,64,1536]{2,1,0:T(8,128)(2,1)} %pad.27) | copy-start | bytes 2359300
  305.9 4.1 copy-start.1
  305.9 5.1 %copy-start.19 = (bf16[4,128,1536]{2,1,0:T(8,128)(2,1)S(1)}, bf16[4,128,1536]{2,1,0:T(8,128)(2,1)}, u32[]{:S(2)}) copy-start(bf16[4,128,1536]{2,1,0:T(8,128)(2,1)} %get-tuple-element.42) | copy-start | bytes 4718596
  391.4 50.1 %copy-start.7 = (f32[128,1536]{1,0:T(8,128)S(1)}, f32[128,1536]{1,0:T(8,128)}, u32[]{:S(2)}) copy-start(f32[128,1536]{1,0:T(8,128)} %get-tuple-element.40.hidden) | copy-start | bytes 2359300
  391.4 50.1 %copy-start.8 = (f32[128,1536]{1,0:T(8,128)S(1)}, f32[128,1536]{1,0:T(8,128)}, u32[]{:S(2)}) copy-start(f32[128,1536]{1,0:T(8,128)} %get-tuple-element.50) | copy-start | bytes 2359300
  391.4 50.1 %copy-start.9 = (f32[128,1536]{1,0:T(8,128)S(1)}, f32[128,1536]{1,0:T(8,128)}, u32[]{:S(2)}) copy-start(f32[128,1536]{1,0:T(8,128)} %get-tuple-element.49) | copy-start | bytes 2359300
  440.2 3.7 copy-start.12
  444.0 2.9 copy-start.10
  444.5 4.2 copy-start.13
  444.5 4.1 copy-start.14
  444.7 5.4 %copy-start.2 = (bf16[8,48,1024]{2,1,0:T(8,128)(2,1)S(1)}, bf16[8,48,1024]{2,1,0:T(8,128)(2,1)}, u32[]{:S(2)}) copy-start(bf16[8,48,1024]{2,1,0:T(8,128)(2,1)} %get-tuple-element.57) | copy-start | bytes 2359300
  452.8 2.5 copy-start.15
  452.8 3.2 copy-start.5

commit v2 on v1

--- a/solution.py
+++ b/solution.py
@@ -522,9 +522,16 @@
 
     def pump(self, t):
         for k in range(CHUNKS):
-            self.copy(t - 1, k).wait_recv()
-            if t < CHIPS - 1:
-                self.copy(t, k).start()
+            self.pass_on(t, k)
+
+    def pass_on(self, t, k):
+        self.copy(t - 1, k).wait_recv()
+        if t < CHIPS - 1:
+            self.copy(t, k).start()
+
+    def pump_some(self, first, last):
+        for n in range(first, last):
+            self.pass_on(1 + n // CHUNKS, n % CHUNKS)
 
     def finish(self):
         for t in range(CHIPS - 1):
@@ -644,72 +651,68 @@
 
 
 class Collect:
-    sems = [pltpu.SemaphoreType.DMA, pltpu.SemaphoreType.DMA, pltpu.SemaphoreType.DMA,
-            pltpu.SemaphoreType.DMA, pltpu.SemaphoreType.DMA((CHIPS,)),
-            pltpu.SemaphoreType.DMA((CHIPS,))]
+    order = tuple(range(1, CHIPS)) + (0,)
+    sems = [pltpu.SemaphoreType.DMA((CHIPS,))] * 6
 
     @staticmethod
     def bufs(rows, columns):
-        return [VMEM((16, rows, columns), BF), VMEM((16, rows, columns), BF),
-                VMEM((8, rows, columns), BF), VMEM((8, rows, columns), BF)]
+        return [VMEM((CHIPS, 2, rows, columns), BF), VMEM((CHIPS, 2, rows, columns), BF),
+                VMEM((CHIPS, rows, columns), BF), VMEM((CHIPS, rows, columns), BF)]
 
     def __init__(self, place, grads, got, bufs, sems):
         self.place, self.grads, self.got = place, grads, got
         self.sib_in, self.pair, self.y_in, self.total = bufs
         self.s1, self.r1, self.s2, self.r2, self.s3, self.r3 = sems
 
-    def sib(self):
+    def sib(self, n):
         p = self.place
-        return remote(self.grads.at[:, 1 - p.core], self.sib_in, self.s1, self.r1, p.sib)
-
-    def y(self):
+        return remote(self.grads.at[:, (p.chip + n) % CHIPS, 1 - p.core], self.sib_in.at[n],
+                      self.s1.at[n], self.r1.at[n], p.sib)
+
+    def y(self, n):
         p = self.place
-        return remote(self.pair.at[pl.ds((1 - p.g) * 8, 8)], self.y_in, self.s2, self.r2, p.ynb)
-
-    def across(self, i):
+        return remote(self.pair.at[n, 1 - p.g], self.y_in.at[n], self.s2.at[n], self.r2.at[n], p.ynb)
+
+    def across(self, n):
         p = self.place
-        return remote(self.total.at[(p.chip + i) % CHIPS], self.got.at[p.chip], self.s3.at[i],
-                      self.r3.at[i], p.off(i))
-
-    def arrived(self, i):
+        return remote(self.total.at[n], self.got.at[p.chip], self.s3.at[n], self.r3.at[n], p.off(n))
+
+    def arrived(self, n):
         p = self.place
-        return remote(self.total.at[0], self.got.at[p.src(i)], self.s3.at[i], self.r3.at[i],
-                      p.off(i))
+        return remote(self.total.at[n], self.got.at[p.src(n)], self.s3.at[n], self.r3.at[n], p.off(n))
 
     def start(self):
-        self.sib().start()
-
-    def mid(self):
-        p = self.place
-        self.sib().wait_recv()
-
-        def add(n, carry):
-            self.pair[n] = (self.grads[n, p.core].astype(F32) + self.sib_in[n].astype(F32)).astype(BF)
-            return carry
-
-        lax.fori_loop(0, 16, add, 0)
-        self.y().start()
-
-    def send(self):
-        p = self.place
-        self.y().wait_recv()
-
-        def add(n, carry):
-            self.total[n] = (self.pair[p.g * 8 + n].astype(F32) + self.y_in[n].astype(F32)).astype(BF)
-            return carry
-
-        lax.fori_loop(0, 8, add, 0)
-        for i in range(1, CHIPS):
-            self.across(i).start()
-        self.got[p.chip] = self.total[p.chip]
+        for n in self.order:
+            self.sib(n).start()
+
+    def pair_up(self, m):
+        p, n = self.place, self.order[m]
+        self.sib(n).wait_recv()
+        for g in range(2):
+            self.pair[n, g] = (self.grads[g, (p.chip + n) % CHIPS, p.core].astype(F32)
+                               + self.sib_in[n, g].astype(F32)).astype(BF)
+        self.y(n).start()
+
+    def send(self, m):
+        p, n = self.place, self.order[m]
+        self.y(n).wait_recv()
+        value = (self.pair[n, p.g].astype(F32) + self.y_in[n].astype(F32)).astype(BF)
+        if n == 0:
+            self.got[p.chip] = value
+        else:
+            self.total[n] = value
+            self.across(n).start()
+
+    def receive(self):
+        for n in range(1, CHIPS):
+            self.arrived(n).wait_recv()
 
     def finish(self):
-        for i in range(1, CHIPS):
-            self.arrived(i).wait_recv()
-        self.sib().wait_send()
-        self.y().wait_send()
-        for i in range(1, CHIPS):
-            self.across(i).wait_send()
+        for n in range(CHIPS):
+            self.sib(n).wait_send()
+            self.y(n).wait_send()
+            if n > 0:
+                self.across(n).wait_send()
 
 
 def dot(a, b):
@@ -752,18 +755,41 @@
     return value.reshape(value.shape[0] * value.shape[1], value.shape[2])
 
 
-def front_kernel(xh, slab, wo, cs, sn, xg, wqkv, wout, q, keys, values, wo2,
-                 ag_s, ag_r, s1, r1, s2, r2, s3, r3, ws, wr, ks, kr, vs, vr, local):
+LOG2E = 1.4426950408889634
+SCALE = 1.0 / math.sqrt(96)
+SCALE2 = SCALE * LOG2E
+
+
+def scores_of(keys, query, limit, j):
+    s = dot_nt(keys[j], query) * SCALE2
+    pos = lax.broadcasted_iota(jnp.int32, s.shape, 0) + j * 256
+    return jnp.where(pos.astype(F32) <= limit, s, neg_big)
+
+
+def front_kernel(xh, slab, wo, cs, sn, limits, bg, slab_gu, wd,
+                 xg, wqkv, wout, q, keys, values, mix, mix_t, stat, bgg, wgu, wdown,
+                 wo2, vt,
+                 ag_s, ag_r, s1, r1, s2, r2, s3, r3, bg_s, bg_r, g1, h1, g2, h2, g3, h3,
+                 ws, wr, ks, kr, vs, vr, ds, dr, local):
     p = Place()
     greet(all_to_all_devices(p) + [p.sib, p.ynb])
     gather = RingGather(p, xg, ag_s, ag_r)
     spread = Spread(p, slab, wqkv, local, s1, r1, s2, r2, s3, r3)
+    gather_bg = RingGather(p, bgg, bg_s, bg_r)
+    spread_gu = Spread(p, slab_gu, wgu, local, g1, h1, g2, h2, g3, h3)
     xg[p.chip] = xh[...]
     gather.start()
     wo2[p.g] = wo[...]
     swap = remote(wo2.at[p.g], wo2.at[p.g], ws.at[0], wr.at[0], p.ynb)
     swap.start()
     spread.start()
+    bgg[p.chip] = bg[...]
+    here = p.g * 2 + p.core
+    there = (1 - p.g) * 2 + p.core
+    wdown[here] = wd[...]
+    d_swap = remote(wdown.at[here], wdown.at[here], ds.at[0], dr.at[0], p.ynb)
+    d_sib = remote(wdown.at[here], wdown.at[here], ds.at[1], dr.at[1], p.sib)
+    d_sib2 = remote(wdown.at[there], wdown.at[there], ds.at[2], dr.at[2], p.sib)
     gather.pump(1)
     remote(wo2.at[1 - p.g], wo2.at[1 - p.g], ws.at[0], wr.at[0], p.ynb).wait_recv()
     mine = p.x * 2 + p.core
@@ -782,91 +808,32 @@
     for t in range(3, CHIPS):
         gather.pump(t)
         spread.pump(t)
+    gather_bg.start()
+    spread_gu.start()
+    d_swap.start()
+    d_sib.start()
     spread.finish()
 
     def kv_copy(i, n):
         ref, send, recv = ((keys, ks, kr), (values, vs, vr))[n]
-        part = ref.at[2 * i + p.core]
+        part = ref.at[i, pl.ds(pl.multiple_of(p.core * TOK, TOK), TOK)]
         return remote(part, part, send.at[i], recv.at[i], p.sib)
 
     def kv_in(i, n):
         ref, send, recv = ((keys, ks, kr), (values, vs, vr))[n]
-        part = ref.at[2 * i + 1 - p.core]
+        part = ref.at[i, pl.ds(pl.multiple_of((1 - p.core) * TOK, TOK), TOK)]
         return remote(part, part, send.at[i], recv.at[i], p.sib)
 
-    def project(i, carry):
+    def project(i):
         lin = dot(xg[i], whole(wqkv))
         cosine, sine = cs[i], sn[i]
         q[i, pl.ds(0, TOK)] = rope(lin[:, 0:128], cosine, sine).astype(BF)
         q[i, pl.ds(TOK, TOK)] = rope(lin[:, 128:256], cosine, sine).astype(BF)
-        keys[2 * i + p.core] = rope(lin[:, 256:384], cosine, sine).astype(BF)
-        values[2 * i + p.core] = lin[:, 384:512].astype(BF)
+        own = pl.ds(pl.multiple_of(p.core * TOK, TOK), TOK)
+        keys[i, own] = rope(lin[:, 256:384], cosine, sine).astype(BF)
+        values[i, own] = lin[:, 384:512].astype(BF)
         kv_copy(i, 0).start()
         kv_copy(i, 1).start()
-        return carry
-
-    lax.fori_loop(0, CHIPS, project, 0)
-    gather.finish()
-    swap.wait_send()
-    to_x.wait_send()
-    to_s.wait_send()
-    to_s2.wait_send()
-    rest = p.x * 2 + 1 - p.core
-    remote(wout.at[rest], wout.at[rest], ws.at[2], wr.at[2], p.sib).wait_recv()
-    rest2 = (1 - p.x) * 2 + 1 - p.core
-    remote(wout.at[rest2], wout.at[rest2], ws.at[3], wr.at[3], p.sib).wait_recv()
-    for i in range(CHIPS):
-        for n in range(2):
-            kv_copy(i, n).wait_send()
-            kv_in(i, n).wait_recv()
-
-
-def front(xh, slab, wo, cs, sn):
-    dma = pltpu.SemaphoreType.DMA
-    return call(
-        front_kernel,
-        (sds(CHIPS, TOK, 1536), sds(32, 48, 512), sds(4, 48, 1536), sds(CHIPS, 2 * TOK, PAD),
-         sds(2 * CHIPS, TOK, PAD), sds(2 * CHIPS, TOK, PAD), sds(2, 48, 1536)),
-        (xh, slab, wo, cs, sn),
-        RingGather.sems + Spread.sems + [dma((4,)), dma((4,))] + [dma((CHIPS,))] * 4 + [dma],
-        1, 2 * 1024 * 1536 * 512, 10 << 20,
-    )
-
-
-LOG2E = 1.4426950408889634
-SCALE = 1.0 / math.sqrt(96)
-SCALE2 = SCALE * LOG2E
-
-
-def scores_of(keys, query, limit, j):
-    s = dot_nt(keys[j], query) * SCALE2
-    pos = lax.broadcasted_iota(jnp.int32, s.shape, 0) + j * 256
-    return jnp.where(pos.astype(F32) <= limit, s, neg_big)
-
-
-def attn_kernel(q, keys, values, limits, bg, slab, wd, mix, mix_t, stat, bgg, wgu, wdown,
-                vt, ag_s, ag_r, s1, r1, s2, r2, s3, r3, ws, wr, local):
-    p = Place()
-    greet(all_to_all_devices(p) + [p.sib, p.ynb])
-    gather = RingGather(p, bgg, ag_s, ag_r)
-    spread = Spread(p, slab, wgu, local, s1, r1, s2, r2, s3, r3)
-    bgg[p.chip] = bg[...]
-    gather.start()
-    spread.start()
-    here = p.g * 2 + p.core
-    there = (1 - p.g) * 2 + p.core
-    wdown[here] = wd[...]
-    swap = remote(wdown.at[here], wdown.at[here], ws.at[0], wr.at[0], p.ynb)
-    swap.start()
-    to_s = remote(wdown.at[here], wdown.at[here], ws.at[1], wr.at[1], p.sib)
-    to_s.start()
-    to_s2 = remote(wdown.at[there], wdown.at[there], ws.at[2], wr.at[2], p.sib)
-
-    def turn(n, carry):
-        vt[n] = values[n].astype(F32).T.astype(BF)
-        return carry
-
-    lax.fori_loop(0, CHIPS, turn, 0)
 
     def attend(i):
         query = q[i]
@@ -893,117 +860,184 @@
         mix[i, :, pl.ds(PAD, PAD)] = out[TOK:]
 
     for i in range(CHIPS):
+        project(i)
+        gather_bg.pump_some(i, i + 1)
+    spread_gu.pump(1)
+    for i in range(CHIPS):
+        for n in range(2):
+            kv_in(i, n).wait_recv()
+        vt[i] = values[i].astype(F32).T.astype(BF)
+    done = CHIPS
+    for i in range(CHIPS):
         attend(i)
-        if i > 0:
-            gather.pump(i)
-            spread.pump(i)
+        gather_bg.pump_some(done, done + (2 if i < 4 else 3))
+        done += 2 if i < 4 else 3
+        if 1 <= i < CHIPS - 1:
+            spread_gu.pump(i + 1)
         if i == 3:
-            remote(wdown.at[there], wdown.at[there], ws.at[0], wr.at[0], p.ynb).wait_recv()
-            to_s2.start()
-    spread.finish()
+            remote(wdown.at[there], wdown.at[there], ds.at[0], dr.at[0], p.ynb).wait_recv()
+            d_sib2.start()
+    spread_gu.finish()
     gather.finish()
-    swap.wait_send()
-    to_s.wait_send()
-    to_s2.wait_send()
-    rest = p.g * 2 + 1 - p.core
-    remote(wdown.at[rest], wdown.at[rest], ws.at[1], wr.at[1], p.sib).wait_recv()
-    rest2 = (1 - p.g) * 2 + 1 - p.core
-    remote(wdown.at[rest2], wdown.at[rest2], ws.at[2], wr.at[2], p.sib).wait_recv()
-
-
-def attend_all(q, keys, values, limits, bg, slab, wd):
+    gather_bg.finish()
+    for copy in (swap, to_x, to_s, to_s2, d_swap, d_sib, d_sib2):
+        copy.wait_send()
+    for n, slot in ((2, p.x), (3, 1 - p.x)):
+        rest = slot * 2 + 1 - p.core
+        remote(wout.at[rest], wout.at[rest], ws.at[n], wr.at[n], p.sib).wait_recv()
+    for n, slot in ((1, p.g), (2, 1 - p.g)):
+        rest = slot * 2 + 1 - p.core
+        remote(wdown.at[rest], wdown.at[rest], ds.at[n], dr.at[n], p.sib).wait_recv()
+    for i in range(CHIPS):
+        for n in range(2):
+            kv_copy(i, n).wait_send()
+
+
+def front(*ins):
     dma = pltpu.SemaphoreType.DMA
     return call(
-        attn_kernel,
-        (sds(CHIPS, TOK, 2 * PAD), sds(CHIPS, PAD, 256, dtype=F32), sds(CHIPS, 1, 256, dtype=F32),
+        front_kernel,
+        (sds(CHIPS, TOK, 1536), sds(32, 48, 512), sds(4, 48, 1536), sds(CHIPS, 2 * TOK, PAD),
+         sds(CHIPS, 2 * TOK, PAD), sds(CHIPS, 2 * TOK, PAD),
+         sds(CHIPS, TOK, 2 * PAD), sds(CHIPS, PAD, 256, dtype=F32), sds(CHIPS, 1, 256, dtype=F32),
          sds(CHIPS, TOK, 1536), sds(32, 48, 1024), sds(4, 128, 1536)),
-        (q, keys, values, limits, bg, slab, wd),
-        [VMEM((CHIPS, PAD, 256), BF)] + RingGather.sems + Spread.sems
-        + [dma((3,)), dma((3,)), dma],
-        2, 2 * 1024 * 2048 * 256, 10 << 20,
-    )
-
-
-def mid_kernel(mix, wout, tokens, hidden, scale, xg, part, out, held, rs_s, rs_r, ag_s, ag_r):
+        ins,
+        [VMEM((2, 48, 1536), BF), VMEM((CHIPS, PAD, 256), BF)]
+        + RingGather.sems + Spread.sems + RingGather.sems + Spread.sems
+        + [dma((4,)), dma((4,))] + [dma((CHIPS,))] * 4 + [dma((3,)), dma((3,)), dma],
+        1, 5 * 10**9, 20 << 20,
+    )
+
+
+def dot_tn(a, b):
+    return lax.dot_general(a, b, (((0,), (0,)), ((), ())), preferred_element_type=F32)
+
+
+def rows_of(k):
+    return pl.ds(k * ROWS, ROWS)
+
+
+def mid_kernel(mix, wout, tokens, wgu, wdown, bgg, hidden, grad, inner, dgu, dwd, grad_rows, dout,
+               x2, gub, low, part, own, scale, out, held, out2, held2,
+               rs_s, rs_r, ag_s, ag_r, rs2_s, rs2_r, ag2_s, ag2_r):
     p = Place()
     greet([p.next, p.prev])
     scatter = RingScatter(p, out, held, rs_s, rs_r)
-    gather = RingGather(p, xg, ag_s, ag_r)
+    gather = RingGather(p, x2, ag_s, ag_r)
+    scatter2 = RingScatter(p, out2, held2, rs2_s, rs2_r)
+    gather2 = RingGather(p, low, ag2_s, ag2_r)
     for t in range(CHIPS):
         part[...] = dot(mix[scatter.dest(t)], wout[...])
         if t < CHIPS - 1:
-            scatter.push(t, lambda k: part[pl.ds(k * ROWS, ROWS)])
+            scatter.push(t, lambda k: part[rows_of(k)])
     for k in range(CHUNKS):
-        rows = pl.ds(k * ROWS, ROWS)
-        h = tokens[rows] + part[rows] + scatter.last(k)
+        rows = rows_of(k)
+        h = tokens[rows].astype(F32) + part[rows] + scatter.last(k)
         r = lax.rsqrt(jnp.mean(h * h, axis=-1, keepdims=True) + epsilon)
         hidden[rows] = h
         scale[rows] = jnp.broadcast_to(r, (ROWS, 128))
-        xg[p.chip, rows] = (h * r).astype(BF)
+        x2[p.chip, rows] = (h * r).astype(BF)
         gather.start(k)
+
+    def feed(b, target):
+        lin = dot(x2[b], wgu[...])
+        gate, up = lin[:, :512], lin[:, 512:]
+        sigma = jax.nn.sigmoid(gate)
+        act = gate * sigma
+        inner[b] = (act * up).astype(BF)
+        back = dot_nt(bgg[b], wdown[...])
+        gub[b, :, pl.ds(0, 512)] = (back * up * (sigma + act * (1.0 - sigma))).astype(BF)
+        gub[b, :, pl.ds(512, 512)] = (back * act).astype(BF)
+        target[...] = dot_nt(gub[b], wgu[...])
+
+    feed(p.chip, own)
     for t in range(1, CHIPS):
         gather.pump(t)
+        feed(p.behind(t), part)
+        scatter2.push(t - 1, lambda k: part[rows_of(k)])
+    for k in range(CHUNKS):
+        rows = rows_of(k)
+        a = own[rows] + scatter2.last(k)
+        h = hidden[rows]
+        r = scale[rows, pl.ds(0, 1)]
+        value = (bgg[p.chip, rows].astype(F32) + r * a
+                 - h * (r * r * r) * jnp.mean(a * h, axis=-1, keepdims=True))
+        grad[rows] = value
+        low[p.chip, rows] = value.astype(BF)
+        gather2.start(k)
+
+    def weight_part(n):
+        if n < 12:
+            cols = pl.ds(n * 128, 128)
+            dgu[cols] = dot_tn(whole(x2.at[:, :, cols]), whole(gub)).astype(BF)
+        else:
+            cols = pl.ds((n - 12) * 128, 128)
+            dwd[cols] = dot_tn(whole(inner.at[:, :, cols]), whole(bgg)).astype(BF)
+
+    def head_part(b):
+        rows = dot_nt(low[b], wout[...]).astype(BF)
+        grad_rows[b, pl.ds(0, TOK)] = rows[:, :PAD]
+        grad_rows[b, pl.ds(TOK, TOK)] = rows[:, PAD:]
+
+    head_part(p.chip)
+    for t in range(1, CHIPS):
+        for n in range(2 * t - 2, 2 * t):
+            weight_part(n)
+        gather2.pump(t)
+        head_part(p.behind(t))
+    weight_part(14)
+    weight_part(15)
+    for n in range(2):
+        cols = pl.ds(n * 128, 128)
+        dout[cols] = dot_tn(whole(mix.at[:, :, cols]), whole(low)).astype(BF)
     scatter.finish()
     gather.finish()
-
-
-def middle(mix, wout, tokens):
+    scatter2.finish()
+    gather2.finish()
+
+
+def middle(mix, wout, tokens, wgu, wdown, bgg):
     return call(
         mid_kernel,
-        (sds(TOK, 1536, dtype=F32), sds(TOK, 128, dtype=F32), sds(CHIPS, TOK, 1536)),
-        (mix, wout, tokens),
-        [VMEM((TOK, 1536), F32)] + RingScatter.bufs + RingScatter.sems + RingGather.sems,
-        3, 2 * 1024 * 256 * 1536, 10 << 20,
-    )
-
-
-def back_kernel(gub, wgu, hidden, scale, bg, grad, low_all, part, out, held, rs_s, rs_r, ag_s, ag_r):
-    p = Place()
-    greet([p.next, p.prev])
-    scatter = RingScatter(p, out, held, rs_s, rs_r)
-    gather = RingGather(p, low_all, ag_s, ag_r)
-    for t in range(CHIPS):
-        part[...] = dot_nt(gub[scatter.dest(t)], wgu[...])
-        if t < CHIPS - 1:
-            scatter.push(t, lambda k: part[pl.ds(k * ROWS, ROWS)])
-    for k in range(CHUNKS):
-        rows = pl.ds(k * ROWS, ROWS)
-        a = part[rows] + scatter.last(k)
-        h = hidden[rows]
-        r = scale[rows, pl.ds(0, 1)]
-        value = bg[rows].astype(F32) + r * a - h * (r * r * r) * jnp.mean(a * h, axis=-1, keepdims=True)
-        grad[rows] = value
-        low_all[p.chip, rows] = value.astype(BF)
-        gather.start(k)
-    for t in range(1, CHIPS):
-        gather.pump(t)
-    scatter.finish()
-    gather.finish()
-
-
-def back(gub, wgu, hidden, scale, bg):
-    return call(
-        back_kernel,
-        (sds(TOK, 1536, dtype=F32), sds(CHIPS, TOK, 1536)),
-        (gub, wgu, hidden, scale, bg),
-        [VMEM((TOK, 1536), F32)] + RingScatter.bufs + RingScatter.sems + RingGather.sems,
-        4, 2 * 1024 * 1024 * 1536, 10 << 20,
-    )
-
-
-def attn_back_kernel(q, keys, values, limits, grad_t, grad, mix_t, stat, cs, sn, branch, dgu, dwd,
-                     back_out, branch_sum, got, dwd_sum,
-                     kt, dk, dv, dkv_low, dkv_in, out, held, sib_in, pair, y_in, total,
-                     d_in, d_pair, d_y,
-                     rs_s, rs_r, c1, c2, c3, c4, c5, c6, ds, dr, xs, xr):
+        (sds(TOK, 1536, dtype=F32), sds(TOK, 1536, dtype=F32), sds(CHIPS, TOK, 512), sds(1536, 1024),
+         sds(512, 1536), sds(CHIPS, 2 * TOK, PAD), sds(256, 1536)),
+        (mix, wout, tokens, wgu, wdown, bgg),
+        [VMEM((CHIPS, TOK, 1536), BF), VMEM((CHIPS, TOK, 1024), BF), VMEM((CHIPS, TOK, 1536), BF),
+         VMEM((TOK, 1536), F32), VMEM((TOK, 1536), F32), VMEM((TOK, 128), F32)]
+        + RingScatter.bufs * 2 + RingScatter.sems + RingGather.sems + RingScatter.sems + RingGather.sems,
+        3, 15 * 10**9, 20 << 20,
+    )
+
+
+def tail_kernel(q, keys, values, limits, grad_rows, mix_t, stat, cs, sn, inner, wdown, hidden, valid, dgu, dwd,
+                xg, wqkv, dout, tokens, grad, w_gate, w_up,
+                result, input_back, got_qkv, dout_sum, d_gate, d_up, gain_sum, dwd_sum,
+                kt, dk, dv, dkv_low, dkv_in, back_out, dqkv, part, out, held, out2, held2,
+                gu1, gu2, gu3, gu4, qk1, qk2, qk3, qk4, got_gu, d_in, d_pair, d_y, o_in, o_pair, o_two, o_y,
+                rs_s, rs_r, rs2_s, rs2_r, a1, a2, a3, a4, a5, a6, c1, c2, c3, c4, c5, c6,
+                ds, dr, xs, xr, os, orr):
     p = Place()
     greet(all_to_all_devices(p) + [p.sib, p.ynb])
     scatter = RingScatter(p, out, held, rs_s, rs_r)
-    collect = Collect(p, dgu, got, (sib_in, pair, y_in, total), (c1, c2, c3, c4, c5, c6))
+    scatter2 = RingScatter(p, out2, held2, rs2_s, rs2_r)
+    collect = Collect(p, dgu, got_gu, (gu1, gu2, gu3, gu4), (a1, a2, a3, a4, a5, a6))
+    collect2 = Collect(p, dqkv, got_qkv, (qk1, qk2, qk3, qk4), (c1, c2, c3, c4, c5, c6))
     collect.start()
     fold = remote(dwd.at[:, 1 - p.core], d_in, ds.at[0], dr.at[0], p.sib)
     fold.start()
-    scatter.push(0, lambda k: branch[scatter.dest(0), pl.ds(k * ROWS, ROWS)].astype(F32))
+    y_fold = remote(d_pair.at[1 - p.g], d_y, ds.at[1], dr.at[1], p.ynb)
+    o_fold = remote(dout.at[:, 1 - p.core], o_in, os.at[0], orr.at[0], p.sib)
+    o_fold.start()
+    x_fold = remote(o_pair.at[1 - p.x], o_two.at[p.x], os.at[1], orr.at[1], p.xnb)
+    x_here = remote(o_pair.at[0], o_two.at[1 - p.x], os.at[1], orr.at[1], p.xnb)
+    oy_fold = remote(o_two.at[1 - p.g], o_y, os.at[2], orr.at[2], p.ynb)
+
+    def branch(t):
+        part[...] = dot(inner[scatter.dest(t)], wdown[...])
+        if t < CHIPS - 1:
+            scatter.push(t, lambda k: part[rows_of(k)])
+
+    branch(0)
 
     def turn(n, carry):
         kt[n] = keys[n].astype(F32).T.astype(BF)
@@ -1016,9 +1050,9 @@
     def attend(i):
         query = q[i]
         limit = limits[i]
-        do = grad[i]
+        do = grad_rows[i]
         lse = stat[i]
-        delta = jnp.sum(grad_t[i].astype(F32) * mix_t[i], axis=0, keepdims=True)
+        delta = jnp.sum(do.astype(F32).T * mix_t[i], axis=0, keepdims=True)
 
         def chunk(j, acc):
             w = jnp.exp2(scores_of(keys, query, limit, j) - lse)
@@ -1034,19 +1068,29 @@
         back_out[i, :, pl.ds(0, PAD)] = rope(dq[:TOK], cosine, sine).astype(BF)
         back_out[i, :, pl.ds(PAD, PAD)] = rope(dq[TOK:], cosine, sine).astype(BF)
 
-    y_fold = remote(d_pair.at[1 - p.g], d_y, ds.at[1], dr.at[1], p.ynb)
+    def fold_pairs():
+        fold.wait_recv()
+        for n in range(2):
+            d_pair[n] = (dwd[n, p.core].astype(F32) + d_in[n].astype(F32)).astype(BF)
+        y_fold.start()
+        o_fold.wait_recv()
+        for n in range(2):
+            o_pair[n] = (dout[n, p.core].astype(F32) + o_in[n].astype(F32)).astype(BF)
+        x_fold.start()
+
+    for m in range(3):
+        collect.pair_up(m)
     for i in range(CHIPS):
         attend(i)
+        if i < 5:
+            collect.pair_up(i + 3)
         if 0 < i < CHIPS - 1:
-            scatter.push(i, lambda k: branch[scatter.dest(i), pl.ds(k * ROWS, ROWS)].astype(F32))
-        if i == 1:
-            fold.wait_recv()
-            for n in range(2):
-                d_pair[n] = (dwd[n, p.core].astype(F32) + d_in[n].astype(F32)).astype(BF)
-            y_fold.start()
-            collect.mid()
-        if i == 3:
-            collect.send()
+            branch(i)
+            collect.send(i - 1)
+        if i == 5:
+            fold_pairs()
+    collect.send(6)
+    collect.send(7)
     for n in range(CHIPS):
         for c in range(2):
             rows = pl.ds(c * TOK, TOK)
@@ -1054,11 +1098,13 @@
             dkv_low[1, n, c] = dv[n, rows].astype(BF)
     swap = remote(dkv_low.at[:, :, 1 - p.core], dkv_in, xs, xr, p.sib)
     swap.start()
+    branch(CHIPS - 1)
     for k in range(CHUNKS):
-        rows = pl.ds(k * ROWS, ROWS)
-        branch_sum[rows] = branch[p.chip, rows].astype(F32) + scatter.last(k)
-    y_fold.wait_recv()
-    dwd_sum[...] = d_pair[p.g].astype(F32) + d_y[...].astype(F32)
+        rows = rows_of(k)
+        result[rows] = (valid[rows] * (hidden[rows] + part[rows] + scatter.last(k))).astype(BF)
+    o_two[p.x] = o_pair[p.x]
+    x_here.wait_recv()
+    oy_fold.start()
     swap.wait_recv()
 
     def keys_back(n, carry):
@@ -1069,80 +1115,73 @@
         return carry
 
     lax.fori_loop(0, CHIPS, keys_back, 0)
+
+    def weight_part(n):
+        value = dot_tn(whole(xg.at[:, :, pl.ds(n * 384, 384)]), whole(back_out)).astype(BF)
+        dqkv[n // 2, pl.ds((n % 2) * 4, 4)] = value.reshape(4, 2, 48, 512)
+
+    for t in range(CHIPS):
+        part[...] = dot_nt(back_out[scatter2.dest(t)], whole(wqkv))
+        if t < CHIPS - 1:
+            scatter2.push(t, lambda k: part[rows_of(k)])
+        if t == 0:
+            for n in range(4):
+                weight_part(n)
+            collect2.start()
+        if 1 <= t <= 4:
+            collect2.pair_up(2 * t - 2)
+            collect2.pair_up(2 * t - 1)
+        if 2 <= t <= 5:
+            collect2.send(2 * t - 4)
+            collect2.send(2 * t - 3)
+        if t == 5:
+            y_fold.wait_recv()
+            dwd_sum[...] = d_pair[p.g].astype(F32) + d_y[...].astype(F32)
+            oy_fold.wait_recv()
+            dout_sum[...] = o_two[p.g].astype(F32) + o_y[...].astype(F32)
+        if t == 6:
+            collect.receive()
+            total = jnp.zeros((48, 128), F32)
+            for chip in range(CHIPS):
+                for g in range(2):
+                    cols = pl.ds(g * 2048 + chip * 256, 256)
+                    for n, (target, weight) in enumerate(((d_gate, w_gate), (d_up, w_up))):
+                        piece = got_gu[chip, :, pl.ds(n * 512 + g * 256, 256)]
+                        target[:, cols] = piece
+                        product = piece.astype(F32) * weight[:, cols].astype(F32)
+                        total = total + product[:, :128] + product[:, 128:]
+            gain_sum[...] = total
+    for k in range(CHUNKS):
+        rows = rows_of(k)
+        c = part[rows] + scatter2.last(k)
+        h = tokens[rows].astype(F32)
+        r = lax.rsqrt(jnp.mean(h * h, axis=-1, keepdims=True) + epsilon)
+        input_back[rows] = (grad[rows] + r * c
+                            - h * (r * r * r) * jnp.mean(c * h, axis=-1, keepdims=True)).astype(BF)
+    collect2.receive()
     collect.finish()
+    collect2.finish()
     scatter.finish()
-    fold.wait_send()
-    y_fold.wait_send()
-    swap.wait_send()
-
-
-def attend_back(q, keys, values, limits, grad_t, grad, mix_t, stat, cs, sn, branch, dgu, dwd):
+    scatter2.finish()
+    for copy in (fold, y_fold, swap, o_fold, x_fold, oy_fold):
+        copy.wait_send()
+
+
+def tail(*ins):
     dma = pltpu.SemaphoreType.DMA
     return call(
-        attn_back_kernel,
-        (sds(CHIPS, TOK, 4 * PAD), sds(TOK, 1536, dtype=F32), sds(CHIPS, 48, 1024),
-         sds(TOK, 1536, dtype=F32)),
-        (q, keys, values, limits, grad_t, grad, mix_t, stat, cs, sn, branch, dgu, dwd),
+        tail_kernel,
+        (sds(TOK, 1536), sds(TOK, 1536), sds(CHIPS, 48, 512), sds(48, 1536, dtype=F32), sds(48, 4096),
+         sds(48, 4096), sds(48, 128, dtype=F32), sds(TOK, 1536, dtype=F32)),
+        ins,
         [VMEM((CHIPS, PAD, 256), BF), VMEM((CHIPS, 256, PAD), F32), VMEM((CHIPS, 256, PAD), F32),
-         VMEM((2, CHIPS, 2, TOK, PAD), BF), VMEM((2, CHIPS, TOK, PAD), BF)]
-        + RingScatter.bufs + Collect.bufs(48, 1024)
-        + [VMEM((2, TOK, 1536), BF), VMEM((2, TOK, 1536), BF), VMEM((TOK, 1536), BF)]
-        + RingScatter.sems + Collect.sems + [dma((2,)), dma((2,)), dma, dma],
-        5, 5 * 1024 * 2048 * 256, 20 << 20,
-    )
-
-
-def last_kernel(grads, wqkv, dqkv, dout, csum, got, dout_sum,
-                part, out, held, sib_in, pair, y_in, total, o_in, o_pair, o_two, o_y,
-                rs_s, rs_r, c1, c2, c3, c4, c5, c6, os, orr):
-    p = Place()
-    greet(all_to_all_devices(p) + [p.sib, p.ynb])
-    scatter = RingScatter(p, out, held, rs_s, rs_r)
-    collect = Collect(p, dqkv, got, (sib_in, pair, y_in, total), (c1, c2, c3, c4, c5, c6))
-    collect.start()
-    fold = remote(dout.at[:, 1 - p.core], o_in, os.at[0], orr.at[0], p.sib)
-    fold.start()
-    x_fold = remote(o_pair.at[1 - p.x], o_two.at[p.x], os.at[1], orr.at[1], p.xnb)
-    x_here = remote(o_pair.at[0], o_two.at[1 - p.x], os.at[1], orr.at[1], p.xnb)
-    y_fold = remote(o_two.at[1 - p.g], o_y, os.at[2], orr.at[2], p.ynb)
-    for t in range(CHIPS):
-        part[...] = dot_nt(grads[scatter.dest(t)], whole(wqkv))
-        if t < CHIPS - 1:
-            scatter.push(t, lambda k: part[pl.ds(k * ROWS, ROWS)])
-        if t == 0:
-            fold.wait_recv()
-            for n in range(2):
-                o_pair[n] = (dout[n, p.core].astype(F32) + o_in[n].astype(F32)).astype(BF)
-            x_fold.start()
-            collect.mid()
-        if t == 1:
-            o_two[p.x] = o_pair[p.x]
-            x_here.wait_recv()
-            y_fold.start()
-        if t == 2:
-            collect.send()
-    for k in range(CHUNKS):
-        rows = pl.ds(k * ROWS, ROWS)
-        csum[rows] = part[rows] + scatter.last(k)
-    y_fold.wait_recv()
-    dout_sum[...] = o_two[p.g].astype(F32) + o_y[...].astype(F32)
-    collect.finish()
-    scatter.finish()
-    fold.wait_send()
-    x_fold.wait_send()
-    y_fold.wait_send()
-
-
-def last(grads, wqkv, dqkv, dout):
-    dma = pltpu.SemaphoreType.DMA
-    return call(
-        last_kernel,
-        (sds(TOK, 1536, dtype=F32), sds(CHIPS, 48, 512), sds(48, 1536, dtype=F32)),
-        (grads, wqkv, dqkv, dout),
-        [VMEM((TOK, 1536), F32)] + RingScatter.bufs + Collect.bufs(48, 512)
-        + [VMEM((2, 48, 1536), BF), VMEM((2, 48, 1536), BF), VMEM((2, 48, 1536), BF), VMEM((48, 1536), BF)]
-        + RingScatter.sems + Collect.sems + [dma((3,)), dma((3,))],
-        6, 2 * 1024 * 512 * 1536, 10 << 20,
+         VMEM((2, CHIPS, 2, TOK, PAD), BF), VMEM((2, CHIPS, TOK, PAD), BF), VMEM((CHIPS, TOK, 4 * PAD), BF),
+         VMEM((2, CHIPS, 2, 48, 512), BF), VMEM((TOK, 1536), F32)]
+        + RingScatter.bufs * 2 + Collect.bufs(48, 1024) + Collect.bufs(48, 512)
+        + [VMEM((CHIPS, 48, 1024), BF), VMEM((2, TOK, 1536), BF), VMEM((2, TOK, 1536), BF), VMEM((TOK, 1536), BF),
+           VMEM((2, 48, 1536), BF), VMEM((2, 48, 1536), BF), VMEM((2, 48, 1536), BF), VMEM((48, 1536), BF)]
+        + RingScatter.sems * 2 + Collect.sems * 2 + [dma((2,)), dma((2,)), dma, dma, dma((3,)), dma((3,))],
+        5, 10 * 10**9, 20 << 20,
     )
 
 
@@ -1189,64 +1228,33 @@
     limit = jnp.minimum(positions, length - 1).astype(F32)
     limits = jnp.concatenate([limit, limit], axis=-1).reshape(CHIPS, 1, 2 * TOK)
 
-    xg, wqkv, wout4, q, keys, values, unused = front(xh, slab_qkv, w_out, cs, sn)
-    keys = keys.reshape(CHIPS, 256, PAD)
-    values = values.reshape(CHIPS, 256, PAD)
-    mix, mix_t, stat, bgg, wgu, wdown = attend_all(q, keys, values, limits, bg, slab_gu, w_down)
+    xg, wqkv, wout4, q, keys, values, mix, mix_t, stat, bgg, wgu, wdown = front(
+        xh, slab_qkv, w_out, cs, sn, limits, bg, slab_gu, w_down)
     wout = jnp.pad(wout4, ((0, 0), (0, 16), (0, 0))).reshape(256, 1536)
     wgu = wgu.reshape(1536, 1024)
     wdown = wdown.reshape(512, 1536)
-    hidden, scale, x2 = middle(mix, wout, tokens)
-
-    x2f = x2.reshape(1024, 1536)
-    bgf = bgg.reshape(1024, 1536)
-    lin = jnp.dot(x2f, wgu, preferred_element_type=F32)
-    gate_lin, up_lin = lin[:, :512], lin[:, 512:]
-    sigma = jax.nn.sigmoid(gate_lin)
-    silu_act = gate_lin * sigma
-    inner = (silu_act * up_lin).astype(BF)
-    inner_grad = jnp.einsum("td,fd->tf", bgf, wdown, preferred_element_type=F32)
-    gate_back = (inner_grad * up_lin * (sigma + gate_lin * sigma * (1.0 - sigma))).astype(BF)
-    up_back = (inner_grad * silu_act).astype(BF)
-    gub = jnp.concatenate([gate_back, up_back], axis=-1)
-    grad, mix_back = back(gub.reshape(CHIPS, TOK, 1024), wgu, hidden, scale, bg)
-    branch = jnp.dot(inner, wdown, preferred_element_type=F32).astype(BF).reshape(CHIPS, TOK, 1536)
-    dgu = jnp.einsum("td,tf->df", x2f, gub, preferred_element_type=F32).astype(BF)
-    dwd = jnp.einsum("tf,td->fd", inner, bgf, preferred_element_type=F32).astype(BF)
-
-    mixb = mix_back.reshape(1024, 1536)
-    attn_back = jnp.einsum("te,de->td", mixb, wout, preferred_element_type=F32).astype(BF)
-    dout = jnp.einsum("td,te->de", mix.reshape(1024, 256), mixb, preferred_element_type=F32).astype(BF)
+    hidden, grad, inner, dgu, dwd, grad_rows, dout = middle(mix, wout, hidden_in[0], wgu, wdown, bgg)
     dout = dout.reshape(2, 2, 64, 1536)[:, :, :48]
-    grad_rows = attn_back.reshape(CHIPS, TOK, 2, PAD).swapaxes(1, 2).reshape(CHIPS, 2 * TOK, PAD)
-    grads, branch_sum, got_gu, dwd_sum = attend_back(
-        q, keys, values, limits, grad_rows.swapaxes(1, 2), grad_rows, mix_t, stat, cs, sn, branch,
-        dgu.reshape(16, 2, 48, 1024), dwd.reshape(2, 2, TOK, 1536))
-    result = (valid * (hidden + branch_sum)).astype(BF)[None]
-    dqkv = jnp.einsum("td,te->de", xg.reshape(1024, 1536), grads.reshape(1024, 512),
-                      preferred_element_type=F32).astype(BF)
-    csum, got_qkv, dout_sum = last(grads, wqkv, dqkv.reshape(16, 2, 48, 512), dout)
-    input_back = grad + r_one * csum - tokens * (r_one * r_one * r_one) * jnp.mean(
-        csum * tokens, axis=-1, keepdims=True)
-
-    got_gu = got_gu.astype(F32)
-    unff = lambda v: v.reshape(8, 48, 2, 256).transpose(1, 2, 0, 3).reshape(48, 4096)
-    d_gate, d_up = unff(got_gu[:, :, :512]), unff(got_gu[:, :, 512:])
+    result, input_back, got_qkv, dout_sum, d_gate, d_up, gain_sum, dwd_sum = tail(
+        q, keys, values, limits, grad_rows, mix_t, stat, cs, sn, inner, wdown, hidden, valid,
+        dgu.reshape(2, CHIPS, 2, 48, 1024), dwd.reshape(2, 2, TOK, 1536), xg, wqkv, dout, hidden_in[0], grad,
+        w_gate, w_up)
+
     got_qkv = by_head(got_qkv).swapaxes(0, 1).astype(F32)
     unpad = lambda v: v.reshape(48, -1, 2, 64)[:, :, :, :48].reshape(48, -1)
     d_q, d_k, d_v = unpad(got_qkv[:, :, :256]), unpad(got_qkv[:, :, 256:384]), unpad(got_qkv[:, :, 384:])
     along = lambda w, d: jnp.sum(w.astype(F32) * d, axis=-1)
     return (
-        result,
-        input_back.astype(BF)[None],
+        result[None],
+        input_back[None],
         along(w_query, d_q) + along(w_key, d_k) + along(w_value, d_v),
         d_q * gain_one,
         d_k * gain_one,
         d_v * gain_one,
         dout_sum,
-        along(w_gate, d_gate) + along(w_up, d_up),
-        d_gate * gain_two,
-        d_up * gain_two,
+        jnp.sum(gain_sum, axis=-1),
+        d_gate.astype(F32) * gain_two,
+        d_up.astype(F32) * gain_two,
         dwd_sum,
     )
 

time: 466 us -> 381 us (0.82)
  Pallas kernels: 380 us -> 344 us
  matrix products: 34.1 us -> 0 us
  other arithmetic: 20.7 us -> 12.8 us
    pallas_call x6 -> x3, Pallas kernels: 380 us -> 344 us  [call(): pl.pallas_call(body, out_shape=outs, in_specs=[VSPEC] * len(ins), out_spe...]
    dot_general x8 -> x0, matrix products: 34.1 us -> none  [the longest x1 6.62 us: plane_device(): lin = jnp.dot(x2f, wgu, preferred_element_type=F32)]
where the time goes in v2:
time: 381 us; the launch traced here: 375 us
  Pallas kernels  344 us (90%)
  local copies, waits for them, and re-layouts  15.8 us (4%)
  other arithmetic  12.8 us (3%)
    pallas_call x3, Pallas kernels, call(): pl.pallas_call(body, out_shape=outs, in_specs=[VSPEC] * len(ins), out_spe...  344 us

profile of v2, /device:TPU:0, one launch (start us, length us, event | category | flops | bytes accessed | tf_op | source)
XLA Modules:
  0.0 375.2 jit_solution(7377022388451227791)
XLA Ops:
  1.4 1.9 multiply_sine_fusion
  3.4 1.0 pad_maximum_fusion.2
  4.5 1.0 pad_maximum_fusion.1
  5.5 0.6 reshape.170.limits
  6.1 0.1 fusion.5
  6.2 0.2 reshape.162
  6.4 0.2 pad.23
  6.6 0.1 reshape.163
  6.8 0.2 reshape.164
  7.0 0.2 pad.24
  7.2 0.1 reshape.165
  7.4 0.4 reshape.161
  7.8 0.4 pad.22
  8.3 0.3 reshape_reshape.3
  8.6 0.1 copy.41
  8.8 0.8 copy.42
  9.5 0.2 fusion
  9.7 1.1 fusion.1
  10.8 0.2 multiply_convert_fusion.1
  11.1 0.3 copy.43
  11.4 0.3 reshape.172
  11.8 0.3 copy.44
  12.1 0.3 reshape.174
  12.3 1.0 pad_maximum_fusion.slab_gu
  13.3 108.4 %shard_map.203 = (bf16[8,128,1536]{2,1,0:T(8,128)(2,1)}, bf16[32,48,512]{2,1,0:T(8,128)(2,1)}, bf16[4,48,1536]{2,1,0:T(8,128)(2,1)}, bf16[8,256,128]{2,1,0:T(8,1...) custom-call(bf16[128,1536]{1,0:T(8,128)(2,1)} %get-tuple-element.87., ...), custom_call_target="tpu_custom_call" | custom-call | flops 5000000000 | bytes 20971520 | tf_op jit(solution)/shard_map/pallas_call | solution.py:734
  121.7 2.0 pad.27
  123.8 135.4 %shard_map.204 = (f32[128,1536]{1,0:T(8,128)}, f32[128,1536]{1,0:T(8,128)}, bf16[8,128,512]{2,1,0:T(8,128)(2,1)}, bf16[1536,1024]{1,0:T(8,128)(2,1)}, bf16[512,1...) custom-call(bf16[8,128,256]{2,1,0:T(8,128)(2,1)} %get-tuple-element.41.mix, ...), custom_call_target="tpu_custom_call" | custom-call | flops 15000000512 | bytes 20971520 | tf_op jit(solution)/shard_map/pallas_call | solution.py:734
  259.2 1.9 slice.28.dout
  261.1 0.6 fusion.9.valid
  261.7 100.6 %shard_map.205 = (bf16[128,1536]{1,0:T(8,128)(2,1)}, bf16[128,1536]{1,0:T(8,128)(2,1)}, bf16[8,48,512]{2,1,0:T(8,128)(2,1)}, f32[48,1536]{1,0:T(8,128)}, bf16[48...) custom-call(bf16[8,256,128]{2,1,0:T(8,128)(2,1)} %get-tuple-element.38.q, ...), custom_call_target="tpu_custom_call" | custom-call | flops 10000000000 | bytes 20971520 | tf_op jit(solution)/shard_map/pallas_call | solution.py:734
  362.3 2.5 convert_multiply_fusion.3
  365.0 0.2 reshape.183
  365.2 0.1 copy.48
  365.4 0.5 reshape.184
  365.9 0.2 reshape.185
  366.2 0.1 copy.49
  366.3 0.5 reshape.186
  366.8 0.9 broadcast_multiply_fusion.1
  367.8 0.2 copy.47
  368.1 0.5 reshape.181
  368.5 1.1 reshape.182
  369.6 0.9 broadcast_multiply_fusion
  370.6 0.5 add_add_fusion
  371.1 0.6 reduce_sum.49
  371.7 0.7 copy.57
  372.5 0.7 copy.58
  373.2 0.7 copy.59
  373.9 0.9 copy.60
  (47 shorter events, 0.7 us)
Async XLA Ops:
  3.4 2.7 copy-start.13
  3.4 2.7 copy-start.9
  3.4 2.7 copy-start.10
  4.4 2.9 copy-start.2
  8.2 1.3 copy-start
  8.3 1.5 copy-start.5
  8.7 2.1 copy-start.14
  8.7 2.1 copy-start.6
  8.7 2.0 copy-start.7
  362.3 2.5 copy-start.8
  368.0 3.1 copy-start.12
  368.0 3.7 copy-start.4
  368.5 3.9 %copy-start.3 = (bf16[128,1536]{1,0:T(8,128)(2,1)S(1)}, bf16[128,1536]{1,0:T(8,128)(2,1)}, u32[]{:S(2)}) copy-start(bf16[128,1536]{1,0:T(8,128)(2,1)} %get-tuple-element.58) | copy-start | bytes 1179652
  368.5 4.7 %copy-start.11 = (f32[48,1536]{1,0:T(8,128)S(1)}, f32[48,1536]{1,0:T(8,128)}, u32[]{:S(2)}) copy-start(f32[48,1536]{1,0:T(8,128)} %get-tuple-element.106) | copy-start | bytes 884740
  369.6 4.3 %copy-start.1 = (f32[128,1536]{1,0:T(8,128)S(1)}, f32[128,1536]{1,0:T(8,128)}, u32[]{:S(2)}) copy-start(f32[128,1536]{1,0:T(8,128)} %get-tuple-element.110) | copy-start | bytes 2359300

commit v3 on v2

--- a/solution.py
+++ b/solution.py
@@ -659,8 +659,8 @@
         return [VMEM((CHIPS, 2, rows, columns), BF), VMEM((CHIPS, 2, rows, columns), BF),
                 VMEM((CHIPS, rows, columns), BF), VMEM((CHIPS, rows, columns), BF)]
 
-    def __init__(self, place, grads, got, bufs, sems):
-        self.place, self.grads, self.got = place, grads, got
+    def __init__(self, place, grads, own, got, bufs, sems):
+        self.place, self.grads, self.own, self.got = place, grads, own, got
         self.sib_in, self.pair, self.y_in, self.total = bufs
         self.s1, self.r1, self.s2, self.r2, self.s3, self.r3 = sems
 
@@ -689,7 +689,7 @@
         p, n = self.place, self.order[m]
         self.sib(n).wait_recv()
         for g in range(2):
-            self.pair[n, g] = (self.grads[g, (p.chip + n) % CHIPS, p.core].astype(F32)
+            self.pair[n, g] = (self.own(g, (p.chip + n) % CHIPS).astype(F32)
                                + self.sib_in[n, g].astype(F32)).astype(BF)
         self.y(n).start()
 
@@ -727,27 +727,89 @@
     return [place.off(i) for i in range(1, CHIPS)]
 
 
-def call(body, outs, ins, scratch, collective_id, flops=0, nbytes=0):
+def call(body, outs, ins, scratch, collective_id, far_ins=(), far_outs=(), flops=0, nbytes=0):
     kwargs = {}
     if collective_id is not None:
         kwargs = dict(collective_id=collective_id, has_side_effects=True)
+    far = pl.BlockSpec(memory_space=pl.ANY)
     return pl.pallas_call(
         body,
         out_shape=outs,
-        in_specs=[VSPEC] * len(ins),
-        out_specs=tuple(VSPEC for _ in outs) if isinstance(outs, (tuple, list)) else VSPEC,
+        in_specs=[far if n in far_ins else VSPEC for n in range(len(ins))],
+        out_specs=tuple(far if n in far_outs else VSPEC for n in range(len(outs))),
         scratch_shapes=scratch,
         compiler_params=pltpu.CompilerParams(vmem_limit_bytes=60 << 20, **kwargs),
         cost_estimate=pl.CostEstimate(flops=flops, bytes_accessed=nbytes, transcendentals=0),
     )(*ins)
 
 
+class Moves:
+    def __init__(self, sems, *pairs):
+        self.copies = [pltpu.make_async_copy(a, b, sems.at[n]) for n, (a, b) in enumerate(pairs)]
+
+    def start(self, *which):
+        for n in which or range(len(self.copies)):
+            self.copies[n].start()
+
+    def wait(self, *which):
+        for n in which or range(len(self.copies)):
+            self.copies[n].wait()
+
+
 def sds(*shape, dtype=BF):
     return jax.ShapeDtypeStruct(shape, dtype)
 
 
 def rope(u, cosine, sine):
     return u * cosine + pltpu.roll(u, 64, 1) * sine
+
+
+def tables(rows, starts, i):
+    c_row, s_row = rows[0], rows[1]
+    c_start, s_start = starts[0, i], starts[1, i]
+    return c_start * c_row - s_start * s_row, s_start * c_row + c_start * s_row
+
+
+def limit_of(p, i, length):
+    lane = lax.broadcasted_iota(jnp.int32, (1, 2 * TOK), 1)
+    slot = jnp.where(lane < TOK, lane, lane - TOK) + (2 * i + p.core) * TOK
+    return jnp.minimum(slot.astype(F32), length - 1.0)
+
+
+def valid_of(p, first, rows, length):
+    slot = lax.broadcasted_iota(jnp.int32, (rows, 1), 0) + p.s * TOK + first
+    return jnp.where(slot.astype(F32) < length, 1.0, 0.0)
+
+
+def spacing():
+    r = lax.broadcasted_iota(jnp.int32, (384, 512), 0)
+    c = lax.broadcasted_iota(jnp.int32, (384, 512), 1)
+    target = r
+    for n in range(1, 8):
+        target = target + jnp.where(r >= 48 * n, 16, 0)
+    return jnp.where(target == c, 1.0, 0.0).astype(BF)
+
+
+def chip_of_head(j):
+    return 2 * (j % LINE) + j // LINE
+
+
+def diagonal(n):
+    return lax.broadcasted_iota(jnp.int32, (n, n), 0) == lax.broadcasted_iota(jnp.int32, (n, n), 1)
+
+
+def to_column(row):
+    n = row.shape[1]
+    return jnp.sum(jnp.where(diagonal(n), jnp.broadcast_to(row, (n, n)), 0.0), axis=1, keepdims=True)
+
+
+def to_row(column):
+    n = column.shape[0]
+    return jnp.sum(jnp.where(diagonal(n), jnp.broadcast_to(column, (n, n)), 0.0), axis=0, keepdims=True)
+
+
+def norm_column(h):
+    return lax.rsqrt(jnp.mean(h * h, axis=-1, keepdims=True) + epsilon)
 
 
 def whole(ref):
@@ -766,31 +828,57 @@
     return jnp.where(pos.astype(F32) <= limit, s, neg_big)
 
 
-def front_kernel(xh, slab, wo, cs, sn, limits, bg, slab_gu, wd,
-                 xg, wqkv, wout, q, keys, values, mix, mix_t, stat, bgg, wgu, wdown,
-                 wo2, vt,
+def front_kernel(tokens, wq, wk, wv, wo, gain_one, rope_rows, rope_starts, length_row, out_grad, wg, wu, gain_two, wd,
+                 xg_out, wqkv_out, wpad_out, q_out, keys_out, values_out, mix_out, mix_t_out, stat_out,
+                 bgg, wgu, wdown,
+                 xg, wqkv, wpad, q, keys, values, mix, mix_t, stat,
+                 slab, slab_gu, bg, wout, wo2, vt,
                  ag_s, ag_r, s1, r1, s2, r2, s3, r3, bg_s, bg_r, g1, h1, g2, h2, g3, h3,
-                 ws, wr, ks, kr, vs, vr, ds, dr, local):
+                 ws, wr, ks, kr, vs, vr, ds, dr, local, move_s):
     p = Place()
-    greet(all_to_all_devices(p) + [p.sib, p.ynb])
     gather = RingGather(p, xg, ag_s, ag_r)
     spread = Spread(p, slab, wqkv, local, s1, r1, s2, r2, s3, r3)
     gather_bg = RingGather(p, bgg, bg_s, bg_r)
     spread_gu = Spread(p, slab_gu, wgu, local, g1, h1, g2, h2, g3, h3)
-    xg[p.chip] = xh[...]
+    here = p.g * 2 + p.core
+    there = (1 - p.g) * 2 + p.core
+    moves = Moves(move_s, (xg, xg_out), (wqkv, wqkv_out), (wpad, wpad_out), (q, q_out), (keys, keys_out),
+                  (values, values_out), (mix, mix_out), (mix_t, mix_t_out), (stat, stat_out),
+                  (bg, bgg.at[p.chip]), (wd, wdown.at[here]))
+    moves.start(10)
+    length = length_row[:, pl.ds(0, 1)]
+    h = tokens[...].astype(F32)
+    xg[p.chip] = (h * norm_column(h)).astype(BF)
+    greet(all_to_all_devices(p) + [p.sib, p.ynb])
     gather.start()
     wo2[p.g] = wo[...]
     swap = remote(wo2.at[p.g], wo2.at[p.g], ws.at[0], wr.at[0], p.ynb)
     swap.start()
+    space = spacing()
+    gain_column = to_column(gain_one[...].astype(F32))
+    gain_column2 = to_column(gain_two[...].astype(F32))
+    for n in range(4):
+        cols = pl.ds(n * 384, 384)
+        wide = dot((wq[:, cols].astype(F32) * gain_column).astype(BF), space).astype(BF)
+        for m in range(2):
+            slab[chip_of_head(2 * n + m), :, pl.ds(0, 256)] = wide[:, m * 256:m * 256 + 256]
+    for n in range(2):
+        for source, place in ((wk, 256), (wv, 384)):
+            wide = dot((source[:, pl.ds(n * 384, 384)].astype(F32) * gain_column).astype(BF), space).astype(BF)
+            for m in range(4):
+                slab[chip_of_head(4 * n + m), :, pl.ds(place, 128)] = wide[:, m * 128:m * 128 + 128]
     spread.start()
-    bgg[p.chip] = bg[...]
-    here = p.g * 2 + p.core
-    there = (1 - p.g) * 2 + p.core
-    wdown[here] = wd[...]
+    bg[...] = (out_grad[...].astype(F32) * valid_of(p, 0, TOK, length)).astype(BF)
+    moves.start(9)
     d_swap = remote(wdown.at[here], wdown.at[here], ds.at[0], dr.at[0], p.ynb)
     d_sib = remote(wdown.at[here], wdown.at[here], ds.at[1], dr.at[1], p.sib)
     d_sib2 = remote(wdown.at[there], wdown.at[there], ds.at[2], dr.at[2], p.sib)
     gather.pump(1)
+    for chip in range(CHIPS):
+        for n, source in enumerate((wg, wu)):
+            for g in range(2):
+                slab_gu[chip, :, pl.ds(n * 512 + g * 256, 256)] = (
+                    source[:, pl.ds(g * 2048 + chip * 256, 256)].astype(F32) * gain_column2).astype(BF)
     remote(wo2.at[1 - p.g], wo2.at[1 - p.g], ws.at[0], wr.at[0], p.ynb).wait_recv()
     mine = p.x * 2 + p.core
     theirs = (1 - p.x) * 2 + p.core
@@ -808,11 +896,14 @@
     for t in range(3, CHIPS):
         gather.pump(t)
         spread.pump(t)
+    moves.start(0)
+    moves.wait(9, 10)
     gather_bg.start()
     spread_gu.start()
     d_swap.start()
     d_sib.start()
     spread.finish()
+    moves.start(1)
 
     def kv_copy(i, n):
         ref, send, recv = ((keys, ks, kr), (values, vs, vr))[n]
@@ -826,7 +917,7 @@
 
     def project(i):
         lin = dot(xg[i], whole(wqkv))
-        cosine, sine = cs[i], sn[i]
+        cosine, sine = tables(rope_rows, rope_starts, i)
         q[i, pl.ds(0, TOK)] = rope(lin[:, 0:128], cosine, sine).astype(BF)
         q[i, pl.ds(TOK, TOK)] = rope(lin[:, 128:256], cosine, sine).astype(BF)
         own = pl.ds(pl.multiple_of(p.core * TOK, TOK), TOK)
@@ -837,7 +928,7 @@
 
     def attend(i):
         query = q[i]
-        limit = limits[i]
+        limit = limit_of(p, i, length)
 
         def chunk(j, state):
             top, total, acc = state
@@ -867,6 +958,7 @@
         for n in range(2):
             kv_in(i, n).wait_recv()
         vt[i] = values[i].astype(F32).T.astype(BF)
+    moves.start(3, 4, 5)
     done = CHIPS
     for i in range(CHIPS):
         attend(i)
@@ -877,35 +969,43 @@
         if i == 3:
             remote(wdown.at[there], wdown.at[there], ds.at[0], dr.at[0], p.ynb).wait_recv()
             d_sib2.start()
+    for n, slot in ((2, p.x), (3, 1 - p.x)):
+        rest = slot * 2 + 1 - p.core
+        remote(wout.at[rest], wout.at[rest], ws.at[n], wr.at[n], p.sib).wait_recv()
+    wpad[...] = jnp.zeros_like(wpad)
+    for n in range(4):
+        wpad[n, pl.ds(0, 48)] = wout[n]
+    moves.start(2, 6, 7, 8)
     spread_gu.finish()
     gather.finish()
     gather_bg.finish()
     for copy in (swap, to_x, to_s, to_s2, d_swap, d_sib, d_sib2):
         copy.wait_send()
-    for n, slot in ((2, p.x), (3, 1 - p.x)):
-        rest = slot * 2 + 1 - p.core
-        remote(wout.at[rest], wout.at[rest], ws.at[n], wr.at[n], p.sib).wait_recv()
     for n, slot in ((1, p.g), (2, 1 - p.g)):
         rest = slot * 2 + 1 - p.core
         remote(wdown.at[rest], wdown.at[rest], ds.at[n], dr.at[n], p.sib).wait_recv()
     for i in range(CHIPS):
         for n in range(2):
             kv_copy(i, n).wait_send()
+    moves.wait(*range(9))
 
 
 def front(*ins):
     dma = pltpu.SemaphoreType.DMA
+    shapes = (((CHIPS, TOK, 1536), BF), ((32, 48, 512), BF), ((4, 64, 1536), BF), ((CHIPS, 2 * TOK, PAD), BF),
+              ((CHIPS, 2 * TOK, PAD), BF), ((CHIPS, 2 * TOK, PAD), BF), ((CHIPS, TOK, 2 * PAD), BF),
+              ((CHIPS, PAD, 256), F32), ((CHIPS, 1, 256), F32))
     return call(
         front_kernel,
-        (sds(CHIPS, TOK, 1536), sds(32, 48, 512), sds(4, 48, 1536), sds(CHIPS, 2 * TOK, PAD),
-         sds(CHIPS, 2 * TOK, PAD), sds(CHIPS, 2 * TOK, PAD),
-         sds(CHIPS, TOK, 2 * PAD), sds(CHIPS, PAD, 256, dtype=F32), sds(CHIPS, 1, 256, dtype=F32),
-         sds(CHIPS, TOK, 1536), sds(32, 48, 1024), sds(4, 128, 1536)),
+        tuple(sds(*shape, dtype=kind) for shape, kind in shapes)
+        + (sds(CHIPS, TOK, 1536), sds(32, 48, 1024), sds(4, 128, 1536)),
         ins,
-        [VMEM((2, 48, 1536), BF), VMEM((CHIPS, PAD, 256), BF)]
+        [VMEM(shape, kind) for shape, kind in shapes]
+        + [VMEM((CHIPS, 48, 512), BF), VMEM((CHIPS, 48, 1024), BF), VMEM((TOK, 1536), BF),
+           VMEM((4, 48, 1536), BF), VMEM((2, 48, 1536), BF), VMEM((CHIPS, PAD, 256), BF)]
         + RingGather.sems + Spread.sems + RingGather.sems + Spread.sems
-        + [dma((4,)), dma((4,))] + [dma((CHIPS,))] * 4 + [dma((3,)), dma((3,)), dma],
-        1, 5 * 10**9, 20 << 20,
+        + [dma((4,)), dma((4,))] + [dma((CHIPS,))] * 4 + [dma((3,)), dma((3,)), dma, dma((11,))],
+        1, far_ins=(13,), far_outs=range(12), flops=5 * 10**9, nbytes=20 << 20,
     )
 
 
@@ -917,10 +1017,14 @@
     return pl.ds(k * ROWS, ROWS)
 
 
-def mid_kernel(mix, wout, tokens, wgu, wdown, bgg, hidden, grad, inner, dgu, dwd, grad_rows, dout,
+def mid_kernel(mix, wout, tokens, wgu_in, wdown_in, bgg_in, hidden_out, grad_out, inner_out, dgu_out, dwd_out, rows_out, dout,
+               hidden, grad, inner, dgu, dwd, grad_rows, wgu, wdown, bgg,
                x2, gub, low, part, own, scale, out, held, out2, held2,
-               rs_s, rs_r, ag_s, ag_r, rs2_s, rs2_r, ag2_s, ag2_r):
+               rs_s, rs_r, ag_s, ag_r, rs2_s, rs2_r, ag2_s, ag2_r, move_s):
     p = Place()
+    moves = Moves(move_s, (wgu_in, wgu), (wdown_in, wdown), (bgg_in, bgg), (hidden, hidden_out), (grad, grad_out),
+                  (inner, inner_out), (dgu, dgu_out), (dwd, dwd_out), (grad_rows, rows_out))
+    moves.start(0, 1, 2)
     greet([p.next, p.prev])
     scatter = RingScatter(p, out, held, rs_s, rs_r)
     gather = RingGather(p, x2, ag_s, ag_r)
@@ -950,6 +1054,8 @@
         gub[b, :, pl.ds(512, 512)] = (back * act).astype(BF)
         target[...] = dot_nt(gub[b], wgu[...])
 
+    moves.start(3)
+    moves.wait(0, 1, 2)
     feed(p.chip, own)
     for t in range(1, CHIPS):
         gather.pump(t)
@@ -979,51 +1085,67 @@
         grad_rows[b, pl.ds(0, TOK)] = rows[:, :PAD]
         grad_rows[b, pl.ds(TOK, TOK)] = rows[:, PAD:]
 
+    moves.start(4, 5)
     head_part(p.chip)
     for t in range(1, CHIPS):
         for n in range(2 * t - 2, 2 * t):
             weight_part(n)
         gather2.pump(t)
         head_part(p.behind(t))
+    moves.start(8)
     weight_part(14)
     weight_part(15)
+    moves.start(6, 7)
     for n in range(2):
-        cols = pl.ds(n * 128, 128)
-        dout[cols] = dot_tn(whole(mix.at[:, :, cols]), whole(low)).astype(BF)
+        value = dot_tn(whole(mix.at[:, :, pl.ds(n * 128, 128)]), whole(low)).astype(BF)
+        dout[2 * n] = value[:48]
+        dout[2 * n + 1] = value[64:112]
+    moves.wait(*range(3, 9))
     scatter.finish()
     gather.finish()
     scatter2.finish()
     gather2.finish()
 
 
-def middle(mix, wout, tokens, wgu, wdown, bgg):
+def middle(*ins):
+    shapes = (((TOK, 1536), F32), ((TOK, 1536), F32), ((CHIPS, TOK, 512), BF), ((1536, 1024), BF), ((512, 1536), BF),
+              ((CHIPS, 2 * TOK, PAD), BF))
     return call(
         mid_kernel,
-        (sds(TOK, 1536, dtype=F32), sds(TOK, 1536, dtype=F32), sds(CHIPS, TOK, 512), sds(1536, 1024),
-         sds(512, 1536), sds(CHIPS, 2 * TOK, PAD), sds(256, 1536)),
-        (mix, wout, tokens, wgu, wdown, bgg),
-        [VMEM((CHIPS, TOK, 1536), BF), VMEM((CHIPS, TOK, 1024), BF), VMEM((CHIPS, TOK, 1536), BF),
-         VMEM((TOK, 1536), F32), VMEM((TOK, 1536), F32), VMEM((TOK, 128), F32)]
-        + RingScatter.bufs * 2 + RingScatter.sems + RingGather.sems + RingScatter.sems + RingGather.sems,
-        3, 15 * 10**9, 20 << 20,
-    )
-
-
-def tail_kernel(q, keys, values, limits, grad_rows, mix_t, stat, cs, sn, inner, wdown, hidden, valid, dgu, dwd,
-                xg, wqkv, dout, tokens, grad, w_gate, w_up,
-                result, input_back, got_qkv, dout_sum, d_gate, d_up, gain_sum, dwd_sum,
+        tuple(sds(*shape, dtype=kind) for shape, kind in shapes) + (sds(4, 48, 1536),),
+        ins,
+        [VMEM(shape, kind) for shape, kind in shapes]
+        + [VMEM((1536, 1024), BF), VMEM((512, 1536), BF), VMEM((CHIPS, TOK, 1536), BF),
+           VMEM((CHIPS, TOK, 1536), BF), VMEM((CHIPS, TOK, 1024), BF), VMEM((CHIPS, TOK, 1536), BF),
+           VMEM((TOK, 1536), F32), VMEM((TOK, 1536), F32), VMEM((TOK, 128), F32)]
+        + RingScatter.bufs * 2 + RingScatter.sems + RingGather.sems + RingScatter.sems + RingGather.sems
+        + [pltpu.SemaphoreType.DMA((9,))],
+        3, far_ins=(3, 4, 5), far_outs=range(6), flops=15 * 10**9, nbytes=20 << 20,
+    )
+
+
+def tail_kernel(q_in, keys_in, values_in, rows_in, mix_t_in, stat_in, inner_in, wdown_in, hidden_in, dgu_far, dwd_far,
+                xg_in, wqkv_in, grad_in, rope_rows, rope_starts, length_row, dout, tokens,
+                result, input_back, got_gu, got_qkv, dout_sum, dwd_sum,
+                q, keys, values, grad_rows, mix_t, stat, inner, wdown, hidden, dgu, dwd, xg, wqkv, grad,
                 kt, dk, dv, dkv_low, dkv_in, back_out, dqkv, part, out, held, out2, held2,
-                gu1, gu2, gu3, gu4, qk1, qk2, qk3, qk4, got_gu, d_in, d_pair, d_y, o_in, o_pair, o_two, o_y,
+                gu1, gu2, gu3, gu4, qk1, qk2, qk3, qk4, d_in, d_pair, d_y, o_in, o_pair, o_two, o_y,
                 rs_s, rs_r, rs2_s, rs2_r, a1, a2, a3, a4, a5, a6, c1, c2, c3, c4, c5, c6,
-                ds, dr, xs, xr, os, orr):
+                ds, dr, xs, xr, os, orr, move_s):
     p = Place()
+    moves = Moves(move_s, (inner_in, inner), (wdown_in, wdown), (q_in, q), (keys_in, keys), (values_in, values),
+                  (rows_in, grad_rows), (mix_t_in, mix_t), (stat_in, stat), (dgu_far.at[:, :, p.core], dgu),
+                  (dwd_far.at[:, p.core], dwd), (hidden_in, hidden), (xg_in, xg), (wqkv_in, wqkv), (grad_in, grad))
+    moves.start()
+    length = length_row[:, pl.ds(0, 1)]
     greet(all_to_all_devices(p) + [p.sib, p.ynb])
     scatter = RingScatter(p, out, held, rs_s, rs_r)
     scatter2 = RingScatter(p, out2, held2, rs2_s, rs2_r)
-    collect = Collect(p, dgu, got_gu, (gu1, gu2, gu3, gu4), (a1, a2, a3, a4, a5, a6))
-    collect2 = Collect(p, dqkv, got_qkv, (qk1, qk2, qk3, qk4), (c1, c2, c3, c4, c5, c6))
+    collect = Collect(p, dgu_far, lambda g, chip: dgu[g, chip], got_gu, (gu1, gu2, gu3, gu4), (a1, a2, a3, a4, a5, a6))
+    collect2 = Collect(p, dqkv, lambda g, chip: dqkv[g, chip, p.core], got_qkv, (qk1, qk2, qk3, qk4),
+                       (c1, c2, c3, c4, c5, c6))
     collect.start()
-    fold = remote(dwd.at[:, 1 - p.core], d_in, ds.at[0], dr.at[0], p.sib)
+    fold = remote(dwd_far.at[:, 1 - p.core], d_in, ds.at[0], dr.at[0], p.sib)
     fold.start()
     y_fold = remote(d_pair.at[1 - p.g], d_y, ds.at[1], dr.at[1], p.ynb)
     o_fold = remote(dout.at[:, 1 - p.core], o_in, os.at[0], orr.at[0], p.sib)
@@ -1037,7 +1159,9 @@
         if t < CHIPS - 1:
             scatter.push(t, lambda k: part[rows_of(k)])
 
+    moves.wait(0, 1)
     branch(0)
+    moves.wait(*range(2, 10))
 
     def turn(n, carry):
         kt[n] = keys[n].astype(F32).T.astype(BF)
@@ -1049,7 +1173,7 @@
 
     def attend(i):
         query = q[i]
-        limit = limits[i]
+        limit = limit_of(p, i, length)
         do = grad_rows[i]
         lse = stat[i]
         delta = jnp.sum(do.astype(F32).T * mix_t[i], axis=0, keepdims=True)
@@ -1064,14 +1188,15 @@
 
         acc = lax.fori_loop(0, i + 1, chunk, jnp.zeros((PAD, 256), F32))
         dq = acc.T * SCALE
-        cosine, sine = cs[i], -sn[i]
+        cosine, sine = tables(rope_rows, rope_starts, i)
+        sine = -sine
         back_out[i, :, pl.ds(0, PAD)] = rope(dq[:TOK], cosine, sine).astype(BF)
         back_out[i, :, pl.ds(PAD, PAD)] = rope(dq[TOK:], cosine, sine).astype(BF)
 
     def fold_pairs():
         fold.wait_recv()
         for n in range(2):
-            d_pair[n] = (dwd[n, p.core].astype(F32) + d_in[n].astype(F32)).astype(BF)
+            d_pair[n] = (dwd[n].astype(F32) + d_in[n].astype(F32)).astype(BF)
         y_fold.start()
         o_fold.wait_recv()
         for n in range(2):
@@ -1099,9 +1224,11 @@
     swap = remote(dkv_low.at[:, :, 1 - p.core], dkv_in, xs, xr, p.sib)
     swap.start()
     branch(CHIPS - 1)
+    moves.wait(*range(10, 14))
     for k in range(CHUNKS):
         rows = rows_of(k)
-        result[rows] = (valid[rows] * (hidden[rows] + part[rows] + scatter.last(k))).astype(BF)
+        result[rows] = (valid_of(p, k * ROWS, ROWS, length)
+                        * (hidden[rows] + part[rows] + scatter.last(k))).astype(BF)
     o_two[p.x] = o_pair[p.x]
     x_here.wait_recv()
     oy_fold.start()
@@ -1109,8 +1236,9 @@
 
     def keys_back(n, carry):
         own = pl.ds(pl.multiple_of(p.core * TOK, TOK), TOK)
+        cosine, sine = tables(rope_rows, rope_starts, n)
         back_out[n, :, pl.ds(2 * PAD, PAD)] = rope(
-            (dk[n, own] + dkv_in[0, n].astype(F32)) * SCALE, cs[n], -sn[n]).astype(BF)
+            (dk[n, own] + dkv_in[0, n].astype(F32)) * SCALE, cosine, -sine).astype(BF)
         back_out[n, :, pl.ds(3 * PAD, PAD)] = (dv[n, own] + dkv_in[1, n].astype(F32)).astype(BF)
         return carry
 
@@ -1136,26 +1264,16 @@
             collect2.send(2 * t - 3)
         if t == 5:
             y_fold.wait_recv()
-            dwd_sum[...] = d_pair[p.g].astype(F32) + d_y[...].astype(F32)
+            dwd_sum[...] = (d_pair[p.g].astype(F32) + d_y[...].astype(F32)).astype(BF)
             oy_fold.wait_recv()
-            dout_sum[...] = o_two[p.g].astype(F32) + o_y[...].astype(F32)
+            dout_sum[...] = (o_two[p.g].astype(F32) + o_y[...].astype(F32)).astype(BF)
         if t == 6:
             collect.receive()
-            total = jnp.zeros((48, 128), F32)
-            for chip in range(CHIPS):
-                for g in range(2):
-                    cols = pl.ds(g * 2048 + chip * 256, 256)
-                    for n, (target, weight) in enumerate(((d_gate, w_gate), (d_up, w_up))):
-                        piece = got_gu[chip, :, pl.ds(n * 512 + g * 256, 256)]
-                        target[:, cols] = piece
-                        product = piece.astype(F32) * weight[:, cols].astype(F32)
-                        total = total + product[:, :128] + product[:, 128:]
-            gain_sum[...] = total
     for k in range(CHUNKS):
         rows = rows_of(k)
         c = part[rows] + scatter2.last(k)
         h = tokens[rows].astype(F32)
-        r = lax.rsqrt(jnp.mean(h * h, axis=-1, keepdims=True) + epsilon)
+        r = norm_column(h)
         input_back[rows] = (grad[rows] + r * c
                             - h * (r * r * r) * jnp.mean(c * h, axis=-1, keepdims=True)).astype(BF)
     collect2.receive()
@@ -1169,94 +1287,104 @@
 
 def tail(*ins):
     dma = pltpu.SemaphoreType.DMA
+    heads = (CHIPS, 2 * TOK, PAD)
+    near = [VMEM(heads, BF)] * 4 + [
+        VMEM((CHIPS, PAD, 256), F32), VMEM((CHIPS, 1, 256), F32), VMEM((CHIPS, TOK, 512), BF), VMEM((512, 1536), BF),
+        VMEM((TOK, 1536), F32), VMEM((2, CHIPS, 48, 1024), BF), VMEM((2, TOK, 1536), BF), VMEM((CHIPS, TOK, 1536), BF),
+        VMEM((32, 48, 512), BF), VMEM((TOK, 1536), F32)]
     return call(
         tail_kernel,
-        (sds(TOK, 1536), sds(TOK, 1536), sds(CHIPS, 48, 512), sds(48, 1536, dtype=F32), sds(48, 4096),
-         sds(48, 4096), sds(48, 128, dtype=F32), sds(TOK, 1536, dtype=F32)),
+        (sds(TOK, 1536), sds(TOK, 1536), sds(CHIPS, 48, 1024), sds(CHIPS, 48, 512), sds(48, 1536), sds(TOK, 1536)),
         ins,
-        [VMEM((CHIPS, PAD, 256), BF), VMEM((CHIPS, 256, PAD), F32), VMEM((CHIPS, 256, PAD), F32),
+        near + [VMEM((CHIPS, PAD, 256), BF), VMEM((CHIPS, 256, PAD), F32), VMEM((CHIPS, 256, PAD), F32),
          VMEM((2, CHIPS, 2, TOK, PAD), BF), VMEM((2, CHIPS, TOK, PAD), BF), VMEM((CHIPS, TOK, 4 * PAD), BF),
          VMEM((2, CHIPS, 2, 48, 512), BF), VMEM((TOK, 1536), F32)]
         + RingScatter.bufs * 2 + Collect.bufs(48, 1024) + Collect.bufs(48, 512)
-        + [VMEM((CHIPS, 48, 1024), BF), VMEM((2, TOK, 1536), BF), VMEM((2, TOK, 1536), BF), VMEM((TOK, 1536), BF),
+        + [VMEM((2, TOK, 1536), BF), VMEM((2, TOK, 1536), BF), VMEM((TOK, 1536), BF),
            VMEM((2, 48, 1536), BF), VMEM((2, 48, 1536), BF), VMEM((2, 48, 1536), BF), VMEM((48, 1536), BF)]
-        + RingScatter.sems * 2 + Collect.sems * 2 + [dma((2,)), dma((2,)), dma, dma, dma((3,)), dma((3,))],
-        5, 10 * 10**9, 20 << 20,
-    )
-
-
-def pad_heads(weight, heads):
-    w = weight.reshape(weight.shape[0], heads, 2, 48)
-    return jnp.pad(w, ((0, 0), (0, 0), (0, 0), (0, 16))).reshape(weight.shape[0], heads, PAD)
-
-
-def by_chip(slab):
-    return slab.reshape((2, LINE) + slab.shape[1:]).swapaxes(0, 1).reshape(slab.shape)
-
-
-def by_head(slab):
-    return slab.reshape((LINE, 2) + slab.shape[1:]).swapaxes(0, 1).reshape(slab.shape)
+        + RingScatter.sems * 2 + Collect.sems * 2 + [dma((2,)), dma((2,)), dma, dma, dma((3,)), dma((3,)), dma((14,))],
+        5, far_ins=range(14), flops=10 * 10**9, nbytes=20 << 20,
+    )
+
+
+def place_kernel(got_gu, got_qkv, dout, dwd, block, back, wq, wk, wv, wg, wu, gain_one, gain_two,
+                 block_out, back_out, d_gain_one, d_q, d_k, d_v, d_out, d_gain_two, d_gate, d_up, d_down):
+    block_out[...] = block[...]
+    back_out[...] = back[...]
+    d_out[...] = dout[...].astype(F32)
+    d_down[...] = dwd[...].astype(F32)
+    space = spacing()
+    gain_column = to_column(gain_one[...].astype(F32))
+    gain_column2 = to_column(gain_two[...].astype(F32))
+    lanes = lambda v: jnp.sum(v, axis=-1, keepdims=True)
+    total = jnp.zeros((48, 1), F32)
+    for n in range(4):
+        cols = pl.ds(n * 384, 384)
+        wide = jnp.concatenate([got_qkv[chip_of_head(2 * n + m), :, pl.ds(0, 256)] for m in range(2)], axis=-1)
+        value = dot_nt(wide, space)
+        total = total + lanes(value * wq[:, cols].astype(F32))
+        d_q[:, cols] = value * gain_column
+    for n in range(2):
+        cols = pl.ds(n * 384, 384)
+        for source, target, place in ((wk, d_k, 256), (wv, d_v, 384)):
+            wide = jnp.concatenate([got_qkv[chip_of_head(4 * n + m), :, pl.ds(place, 128)] for m in range(4)], axis=-1)
+            value = dot_nt(wide, space)
+            total = total + lanes(value * source[:, cols].astype(F32))
+            target[:, cols] = value * gain_column
+    d_gain_one[...] = to_row(total)
+    total = jnp.zeros((48, 256), F32)
+    for chip in range(CHIPS):
+        for g in range(2):
+            cols = pl.ds(g * 2048 + chip * 256, 256)
+            for n, (target, weight) in enumerate(((d_gate, wg), (d_up, wu))):
+                piece = got_gu[chip, :, pl.ds(n * 512 + g * 256, 256)].astype(F32)
+                target[:, cols] = piece * gain_column2
+                total = total + piece * weight[:, cols].astype(F32)
+    d_gain_two[...] = to_row(lanes(total))
+
+
+def place_all(*ins):
+    f = lambda *shape: sds(*shape, dtype=F32)
+    return call(
+        place_kernel,
+        (sds(TOK, 1536), sds(TOK, 1536), f(1, 48), f(48, 1536), f(48, 768), f(48, 768), f(48, 1536), f(1, 48), f(48, 4096),
+         f(48, 4096), f(TOK, 1536)),
+        ins, [], None, nbytes=10 << 20,
+    )
 
 
 def plane_device(hidden_in, lengths, attn_gain, w_query, w_key, w_value, w_out, mlp_gain, w_gate, w_up,
                  w_down, out_grad):
     core = lax.axis_index("seq") % 2
-    length = lengths[0]
-    gain_one = attn_gain.astype(F32)[:, None]
-    gain_two = mlp_gain.astype(F32)[:, None]
-    tokens = hidden_in[0].astype(F32)
-    r_one = norm_scale(tokens)
-    xh = (tokens * r_one).astype(BF)
-    own_pos = lax.axis_index("seq") * TOK + jnp.arange(TOK, dtype=jnp.int32)
-    valid = (own_pos < length).astype(F32)[:, None]
-    bg = (valid * out_grad[0].astype(F32)).astype(BF)
-
-    scaled = lambda w, gain: (w.astype(F32) * gain).astype(BF)
-    wq = pad_heads(scaled(w_query, gain_one), 16).reshape(48, 8, 2 * PAD)
-    wk = pad_heads(scaled(w_key, gain_one), 8)
-    wv = pad_heads(scaled(w_value, gain_one), 8)
-    slab_qkv = by_chip(jnp.concatenate([wq, wk, wv], axis=-1).swapaxes(0, 1))
-    ff = lambda w: scaled(w, gain_two).reshape(48, 2, 8, 256).transpose(2, 0, 1, 3).reshape(8, 48, 512)
-    slab_gu = jnp.concatenate([ff(w_gate), ff(w_up)], axis=-1)
-
-    positions = (2 * jnp.arange(CHIPS, dtype=jnp.int32)[:, None] + core) * TOK + jnp.arange(TOK, dtype=jnp.int32)
-    cosine, sine = rope_tables(positions.reshape(-1))
-    cosine = jnp.pad(cosine, ((0, 0), (0, 16)))
-    sine = jnp.pad(sine, ((0, 0), (0, 16)))
-    cs = jnp.concatenate([cosine, cosine], axis=-1).reshape(CHIPS, TOK, PAD)
-    sn = jnp.concatenate([-sine, sine], axis=-1).reshape(CHIPS, TOK, PAD)
-    limit = jnp.minimum(positions, length - 1).astype(F32)
-    limits = jnp.concatenate([limit, limit], axis=-1).reshape(CHIPS, 1, 2 * TOK)
-
-    xg, wqkv, wout4, q, keys, values, mix, mix_t, stat, bgg, wgu, wdown = front(
-        xh, slab_qkv, w_out, cs, sn, limits, bg, slab_gu, w_down)
-    wout = jnp.pad(wout4, ((0, 0), (0, 16), (0, 0))).reshape(256, 1536)
-    wgu = wgu.reshape(1536, 1024)
-    wdown = wdown.reshape(512, 1536)
-    hidden, grad, inner, dgu, dwd, grad_rows, dout = middle(mix, wout, hidden_in[0], wgu, wdown, bgg)
-    dout = dout.reshape(2, 2, 64, 1536)[:, :, :48]
-    result, input_back, got_qkv, dout_sum, d_gate, d_up, gain_sum, dwd_sum = tail(
-        q, keys, values, limits, grad_rows, mix_t, stat, cs, sn, inner, wdown, hidden, valid,
-        dgu.reshape(2, CHIPS, 2, 48, 1024), dwd.reshape(2, 2, TOK, 1536), xg, wqkv, dout, hidden_in[0], grad,
-        w_gate, w_up)
-
-    got_qkv = by_head(got_qkv).swapaxes(0, 1).astype(F32)
-    unpad = lambda v: v.reshape(48, -1, 2, 64)[:, :, :, :48].reshape(48, -1)
-    d_q, d_k, d_v = unpad(got_qkv[:, :, :256]), unpad(got_qkv[:, :, 256:384]), unpad(got_qkv[:, :, 384:])
-    along = lambda w, d: jnp.sum(w.astype(F32) * d, axis=-1)
-    return (
-        result[None],
-        input_back[None],
-        along(w_query, d_q) + along(w_key, d_k) + along(w_value, d_v),
-        d_q * gain_one,
-        d_k * gain_one,
-        d_v * gain_one,
-        dout_sum,
-        jnp.sum(gain_sum, axis=-1),
-        d_gate.astype(F32) * gain_two,
-        d_up.astype(F32) * gain_two,
-        dwd_sum,
-    )
+    gain_one = attn_gain[None]
+    gain_two = mlp_gain[None]
+    tokens = hidden_in[0]
+    length_row = jnp.broadcast_to(lengths.astype(F32)[:, None], (1, 128))
+
+    entry = jnp.arange(PAD, dtype=jnp.int32) % 64
+    used = entry < HD // 2
+    frequency = jnp.where(used, jnp.exp(-math.log(rope_base) * (2.0 * entry.astype(F32) / HD)), 0.0)
+    sign = jnp.where(jnp.arange(PAD) < 64, -1.0, 1.0)
+
+    def both(slots):
+        angles = slots.astype(F32)[:, None] * frequency[None, :]
+        return jnp.stack([jnp.cos(angles), jnp.sin(angles) * sign])
+
+    rope_rows = both(jnp.arange(TOK, dtype=jnp.int32))
+    rope_starts = both((2 * jnp.arange(CHIPS, dtype=jnp.int32) + core) * TOK)[:, :, None]
+
+    xg, wqkv, wpad, q, keys, values, mix, mix_t, stat, bgg, wgu, wdown = front(
+        tokens, w_query, w_key, w_value, w_out, gain_one, rope_rows, rope_starts, length_row, out_grad[0],
+        w_gate, w_up, gain_two, w_down)
+    hidden, grad, inner, dgu, dwd, grad_rows, dout = middle(
+        mix, wpad.reshape(256, 1536), tokens, wgu.reshape(1536, 1024), wdown.reshape(512, 1536), bgg)
+    block, back, got_gu, got_qkv, dout_sum, dwd_sum = tail(
+        q, keys, values, grad_rows, mix_t, stat, inner, wdown.reshape(512, 1536), hidden,
+        dgu.reshape(2, CHIPS, 2, 48, 1024), dwd.reshape(2, 2, TOK, 1536), xg, wqkv, grad,
+        rope_rows, rope_starts, length_row, dout.reshape(2, 2, 48, 1536), tokens)
+    block, back, d_gain_one, d_q, d_k, d_v, d_out, d_gain_two, d_gate, d_up, d_down = place_all(
+        got_gu, got_qkv, dout_sum, dwd_sum, block, back, w_query, w_key, w_value, w_gate, w_up, gain_one, gain_two)
+    return (block[None], back[None], d_gain_one[0], d_q, d_k, d_v, d_out, d_gain_two[0], d_gate, d_up, d_down)
 
 
 def solution(mesh):

time: 381 us -> 345 us (0.906)
  local copies, waits for them, and re-layouts: 15.8 us -> 0.51 us
  other arithmetic: 12.8 us -> 1.71 us
  Pallas kernels: 344 us -> 336 us
    pallas_call x3 -> x4, Pallas kernels: 344 us -> 336 us  [call(): pl.pallas_call(body, out_shape=outs, in_specs=[far if n in far_ins else V...]
    reshape x14 -> x0, local copies, waits for them, and re-layouts: 5.31 us -> none  [the longest x6 3.14 us: plane_device(): unpad = lambda v: v.reshape(48, -1, 2, 64)[:, :, :, :48].reshape(48, -1)]
    mul x4 -> x0, other arithmetic: 4.33 us -> none  [the longest x1 2.5 us: plane_device(): d_up.astype(F32) * gain_two]
where the time goes in v3:
time: 345 us; the launch traced here: 339 us
  Pallas kernels  336 us (97%)
    pallas_call x4, Pallas kernels, call(): pl.pallas_call(body, out_shape=outs, in_specs=[far if n in far_ins else V...  336 us

profile of v3, /device:TPU:0, one launch (start us, length us, event | category | flops | bytes accessed | tf_op | source)
XLA Modules:
  0.0 339.5 jit_solution(494148382200039059)
XLA Ops:
  1.3 0.5 broadcast_in_dim.47.length_row
  1.8 0.1 multiply_cosine_fusion.1
  1.9 0.6 pad_maximum_fusion.1
  2.6 0.3 multiply_cosine_fusion
  2.9 0.7 pad_maximum_fusion.rope_rows
  3.5 104.4 %shard_map.203 = (bf16[8,128,1536]{2,1,0:T(8,128)(2,1)}, bf16[32,48,512]{2,1,0:T(8,128)(2,1)}, bf16[4,64,1536]{2,1,0:T(8,128)(2,1)}, bf16[8,256,128]{2,1,0:T(8,1...) custom-call(bf16[128,1536]{1,0:T(8,128)(2,1)} %bitcast.23, ...), custom_call_target="tpu_custom_call" | custom-call | flops 5000000000 | bytes 20971520 | tf_op jit(solution)/shard_map/pallas_call | solution.py:735
  107.9 131.5 %shard_map.204 = (f32[128,1536]{1,0:T(8,128)}, f32[128,1536]{1,0:T(8,128)}, bf16[8,128,512]{2,1,0:T(8,128)(2,1)}, bf16[1536,1024]{1,0:T(8,128)(2,1)}, bf16[512,1...) custom-call(bf16[8,128,256]{2,1,0:T(8,128)(2,1)} %get-tuple-element.50.mix, ...), custom_call_target="tpu_custom_call" | custom-call | flops 15000000512 | bytes 20971520 | tf_op jit(solution)/shard_map/pallas_call | solution.py:735
  239.5 94.9 %shard_map.205 = (bf16[128,1536]{1,0:T(8,128)(2,1)}, bf16[128,1536]{1,0:T(8,128)(2,1)}, bf16[8,48,1024]{2,1,0:T(8,128)(2,1)}, bf16[8,48,512]{2,1,0:T(8,128)(2,1)...) custom-call(bf16[8,256,128]{2,1,0:T(8,128)(2,1)} %get-tuple-element.47.q_in, ...), custom_call_target="tpu_custom_call" | custom-call | flops 10000000000 | bytes 20971520 | tf_op jit(solution)/shard_map/pallas_call | solution.py:735
  334.4 4.9 %shard_map.206 = (bf16[128,1536]{1,0:T(8,128)(2,1)}, bf16[128,1536]{1,0:T(8,128)(2,1)}, f32[1,48]{1,0:T(1,128)}, f32[48,1536]{1,0:T(8,128)}, f32[48,768]{1,0:T(8...) custom-call(bf16[8,48,1024]{2,1,0:T(8,128)(2,1)} %get-tuple-element., ...), custom_call_target="tpu_custom_call" | custom-call | bytes 10485760 | tf_op jit(solution)/shard_map/pallas_call | solution.py:735
  (3 shorter events, 0.0 us)
